TPU v7x, 512 devices: a whole 4x8x8 slice. The times are simulated.
512 devices in a mesh: fiber: 32 (over y, x), tm: 16 (over z, core).
Axes of the slice: x: 4, y: 8, z: 8, core: 2. Of those that a mesh axis runs over, the one named last changes fastest.
Arguments:
- strain: bfloat16 [1024, 65536], P('tm', 'fiber'), may hold values from -6 to 6
- fan_cut: int32 [64], replicated, may hold values from 0 to 32768
- sta_len: int32 [65536], P('fiber'), may hold values from 8 to 64
- lta_len: int32 [65536], P('fiber'), may hold values from 128 to 2048
- drift_code: int32 [65536], P('fiber'), may hold values from 0 to 64
- threshold: int32 [65536], P('fiber'), may hold values from 16 to 128
Outputs:
- filtered: bfloat16 [1024, 65536], P('tm', 'fiber')
- ratio: float32 [1024, 65536], P('tm', 'fiber')
- ph: float32 [1024, 65536], P('tm', 'fiber')
All inputs are finite; a program needn't handle non-finite values.
Results may differ from a plain program's by a relative error of at most 0.0029.
Values may be sent and summed in bfloat16 or wider, within the bound.
A program may use at most 192 MiB of HBM per device.

v0:
```python
import math

import jax
import jax.numpy as jnp
from jax import lax
from jax.sharding import PartitionSpec as P

FRAME = 128


HIGH = lax.Precision.HIGHEST


def passed_along(block, axis, distance):
    devices = range(lax.axis_size(axis))
    route = [(i - distance, i) for i in devices if i - distance in devices]
    return lax.ppermute(block, axis, route)


def partner_2(array, axis, apart):
    return lax.ppermute(array, axis, [(i, i ^ 1 << apart) for i in range(lax.axis_size(axis))])


def entering(array, axis, combine, identity):
    length, here = (lax.axis_size(axis), lax.axis_index(axis))
    everything = jax.tree.map(lambda part: lax.all_gather(part, axis), array)
    start = jax.tree.map(
        lambda part, zero: jnp.broadcast_to(jnp.asarray(zero, part.dtype), part.shape),
        array,
        identity,
    )

    def lap(k, before):
        reached = k < here
        new = combine(before, jax.tree.map(lambda part: part[k], everything))
        return jax.tree.map(lambda a, b: jnp.where(reached, a, b), new, before)

    return lax.fori_loop(0, length, lap, start)


def time_tables(frame):
    stride = frame // 2
    samples = jnp.arange(frame, dtype=jnp.int32)
    bin_index = jnp.arange(stride, dtype=jnp.int32)
    window = 0.5 - 0.5 * jnp.cos(2.0 * math.pi / frame * samples.astype(jnp.float32))
    angles = (
        2.0 * math.pi / frame * (samples[:, None] * bin_index[None, :] % frame).astype(jnp.float32)
    )
    analysis = jnp.stack([window[:, None] * jnp.cos(angles), -window[:, None] * jnp.sin(angles)])
    weights = jnp.where(bin_index == 0, 1.0, 2.0).astype(jnp.float32) / frame
    synthesis = jnp.stack(
        [weights[:, None] * jnp.cos(angles.T), -weights[:, None] * jnp.sin(angles.T)]
    )
    return (analysis, synthesis)


def dft_block(length, sign):
    indices = jnp.arange(length, dtype=jnp.int32)
    angles = (
        sign
        * 2.0
        * math.pi
        / length
        * (indices[:, None] * indices[None, :] % length).astype(jnp.float32)
    )
    cosine = jnp.cos(angles)
    sine = jnp.sin(angles)
    return jnp.stack([jnp.stack([cosine, -sine]), jnp.stack([sine, cosine])])


def complex_scale(source, cos_part, sin_part):
    real_part = source[0]
    imag_part = source[1]
    return jnp.stack(
        [cos_part * real_part - sin_part * imag_part, cos_part * imag_part + sin_part * real_part]
    )


def grid_angles(outer_len, inner_len, sign):
    total_len = outer_len * inner_len
    outer_idx = jnp.arange(outer_len, dtype=jnp.int32)[:, None]
    inner_idx = jnp.arange(inner_len, dtype=jnp.int32)[None, :]
    return (
        sign * 2.0 * math.pi / total_len * (outer_idx * inner_idx % total_len).astype(jnp.float32)
    )


def grid_shape(total_len):
    inner_len = math.gcd(total_len, 256)
    return (total_len // inner_len, inner_len)


def local_forward(values):
    items, total_len = (values.shape[1], values.shape[2])
    outer_len, inner_len = grid_shape(total_len)
    grid = values.reshape(2, items, outer_len, inner_len)
    grid = jnp.einsum("stka,tqab->sqkb", dft_block(outer_len, -1.0), grid, precision=HIGH)
    angles = grid_angles(outer_len, inner_len, -1.0)
    grid = complex_scale(grid, jnp.cos(angles), jnp.sin(angles))
    return jnp.einsum("stlb,tqkb->sqkl", dft_block(inner_len, -1.0), grid, precision=HIGH)


def local_inverse(grid):
    items, outer_len, inner_len = (grid.shape[1], grid.shape[2], grid.shape[3])
    grid = jnp.einsum("stbl,tqkl->sqkb", dft_block(inner_len, 1.0), grid, precision=HIGH)
    angles = grid_angles(outer_len, inner_len, 1.0)
    grid = complex_scale(grid, jnp.cos(angles), jnp.sin(angles))
    grid = jnp.einsum("stak,tqkb->sqab", dft_block(outer_len, 1.0), grid, precision=HIGH)
    return grid.reshape(2, items, outer_len * inner_len)


def bit_reverse(position, width):
    result = jnp.zeros_like(position)
    for place in range(width):
        result = result + ((position >> place & 1) << width - 1 - place)
    return result


def body(strain, fan_cut, sta_len, lta_len, drift_code, threshold):
    time_dev, chan_dev = strain.shape
    stride = FRAME // 2
    frames_dev = time_dev // stride
    items = frames_dev * stride
    fiber_count = lax.axis_size("fiber")
    channels_all = chan_dev * fiber_count
    fiber_pos = lax.axis_index("fiber")
    analysis, synthesis = time_tables(FRAME)
    rim_rows = passed_along(strain, "tm", 1)
    extended = jnp.concatenate([rim_rows, strain], axis=0).astype(jnp.float32)
    extended = extended.reshape(frames_dev + 1, stride, chan_dev)
    framed = jnp.concatenate([extended[:-1], extended[1:]], axis=1)
    spectrum = jnp.einsum("inc,snb->sibc", framed, analysis, precision=HIGH).reshape(
        2, items, chan_dev
    )
    bit_count = fiber_count.bit_length() - 1
    values = spectrum
    for place in reversed(range(bit_count)):
        distance = 1 << place
        is_upper = fiber_pos >> place & 1 == 1
        partner = partner_2(values, "fiber", place)
        summed = jnp.where(is_upper, partner - values, values + partner)
        angles = -math.pi / distance * (fiber_pos & distance - 1).astype(jnp.float32)
        cos_part = jnp.where(is_upper, jnp.cos(angles), 1.0)
        sin_part = jnp.where(is_upper, jnp.sin(angles), 0.0)
        values = complex_scale(summed, cos_part, sin_part)
    wave_class = bit_reverse(fiber_pos, bit_count)
    channel_idx = jnp.arange(chan_dev, dtype=jnp.int32)
    turn = (
        2.0 * math.pi / channels_all * (channel_idx * wave_class % channels_all).astype(jnp.float32)
    )
    values = complex_scale(values, jnp.cos(turn), -jnp.sin(turn))
    waves = local_forward(values)
    outer_len, inner_len = (waves.shape[2], waves.shape[3])
    outer_idx = jnp.arange(outer_len, dtype=jnp.int32)[:, None]
    inner_idx = jnp.arange(inner_len, dtype=jnp.int32)[None, :]
    wavenum = wave_class + fiber_count * (outer_idx + outer_len * inner_idx)
    wavenum = jnp.minimum(wavenum, channels_all - wavenum)
    cut_items = jnp.tile(fan_cut, frames_dev)
    passband = jnp.where(
        wavenum[None, :, :] <= cut_items[:, None, None], 1.0 / channels_all, 0.0
    ).astype(jnp.float32)
    kept_wave = waves * passband
    values = local_inverse(kept_wave)
    values = complex_scale(values, jnp.cos(turn), jnp.sin(turn))
    for place in range(bit_count):
        distance = 1 << place
        is_upper = fiber_pos >> place & 1 == 1
        angles = math.pi / distance * (fiber_pos & distance - 1).astype(jnp.float32)
        cos_part = jnp.where(is_upper, jnp.cos(angles), 1.0)
        sin_part = jnp.where(is_upper, jnp.sin(angles), 0.0)
        outgoing = complex_scale(values, cos_part, sin_part)
        incoming = partner_2(outgoing, "fiber", place)
        values = jnp.where(is_upper, incoming - outgoing, outgoing + incoming)
    restored = values.reshape(2, frames_dev, stride, chan_dev)
    pieces = jnp.einsum("sibc,sbn->inc", restored, synthesis, precision=HIGH)
    spill = passed_along(pieces[0, :stride], "tm", -1)
    heads = jnp.concatenate([pieces[1:, :stride], spill[None]], axis=0)
    filtered = (pieces[:, stride:] + heads).reshape(time_dev, chan_dev).astype(jnp.bfloat16)
    energy = filtered.astype(jnp.float32) ** 2
    lengths = jnp.stack([sta_len, lta_len]).astype(jnp.float32)
    keep_rate = 1.0 - 1.0 / lengths
    gains = jnp.broadcast_to(keep_rate[:, None, :], (2, time_dev, chan_dev))
    inputs = (1.0 - keep_rate)[:, None, :] * energy[None]

    def affine(early, late):
        return (early[0] * late[0], late[0] * early[1] + late[1])

    run_gain, run_input = lax.associative_scan(affine, (gains, inputs), axis=1)
    unit_pair = jnp.ones((2, chan_dev), jnp.float32)
    zero_pair = jnp.zeros((2, chan_dev), jnp.float32)
    prior_gain, prior_input = entering(
        (run_gain[:, -1], run_input[:, -1]), "tm", affine, (unit_pair, zero_pair)
    )
    starting = prior_gain + prior_input
    levels = run_gain * starting[:, None, :] + run_input
    ratio = levels[0] / levels[1]
    drift_rate = 0.5 + drift_code.astype(jnp.float32) / 64.0
    steps_up = ratio - drift_rate[None, :]
    time_idx = jnp.arange(time_dev, dtype=jnp.int32)
    triangle = (time_idx[None, :] <= time_idx[:, None]).astype(jnp.float32)
    climb_local = jnp.dot(triangle, steps_up, precision=HIGH)
    floor_local = lax.cummin(climb_local, axis=0)

    def drift_pair(early, late):
        return (early[0] + late[0], jnp.minimum(early[1], early[0] + late[1]))

    zero_vec = jnp.zeros((chan_dev,), jnp.float32)
    high_vec = jnp.full((chan_dev,), jnp.inf, jnp.float32)
    prior_sum, prior_low = entering(
        (climb_local[-1], floor_local[-1]), "tm", drift_pair, (zero_vec, high_vec)
    )
    base_low = jnp.minimum(prior_low, 0.0)
    climb = prior_sum[None, :] + climb_local
    lowest = jnp.minimum(base_low[None, :], prior_sum[None, :] + floor_local)
    limits = threshold.astype(jnp.float32)
    ph = (climb - lowest) / limits[None, :]
    return (filtered, ratio, ph)


def solution(mesh):
    return jax.shard_map(
        body,
        mesh=mesh,
        in_specs=(P("tm", "fiber"), P(), P("fiber"), P("fiber"), P("fiber"), P("fiber")),
        out_specs=(P("tm", "fiber"), P("tm", "fiber"), P("tm", "fiber")),
        check_vma=False,
    )
```

profile of v0, /device:TPU:1, one launch (start us, length us, event | category | flops | bytes accessed | tf_op | source)
XLA Modules:
  0.0 493.2 jit_solution(332782806991310320)
XLA Ops:
  0.6 5.4 %collective-permute-start = (bf16[64,2048]{1,0:T(8,128)(2,1)}, bf16[64,2048]{1,0:T(8,128)(2,1)S(1)}, u32[]{:S(2)}, u32[]{:S(2)}) collective-permute-start(bf16[64,2048]{1,0:T(8,128)(2,1)} %param.10), channel_id=1, source_target_pairs={{0,1},{1,2},{2,3},{3,4},{4,5},{5,6},{6,7},{7,8},{8,9},{9,10},{10,1... | collective-permute-start | bytes 786440 | tf_op jit(solution)/shard_map/ppermute | solution.py:17
  6.3 3.7 collective-permute-done
  12.2 7.1 %collective-permute-start.1 = (f32[2,64,2048]{2,1,0:T(8,128)S(1)}, f32[2,64,2048]{2,1,0:T(8,128)S(1)}, u32[]{:S(2)}, u32[]{:S(2)}) collective-permute-start(f32[2,64,2048]{2,1,0:T(8,128)S(1)} %fusion.3), channel_id=1, source_target_pairs={{0,256},{16,272},{32,288},{48,304},{64,320},{80,336},{96,352},{112... | collective-permute-start | bytes 3145736 | tf_op jit(solution)/shard_map/ppermute | solution.py:21
  19.4 45.5 %collective-permute-done.1 = f32[2,64,2048]{2,1,0:T(8,128)S(1)} collective-permute-done((f32[2,64,2048]{2,1,0:T(8,128)S(1)}, f32[2,64,2048]{2,1,0:T(8,128)S(1)}, u32[]{:S(2)}, u32[]{:S(2)}) %collective-permute-start.1) | collective-permute-done | bytes 1048608 | tf_op jit(solution)/shard_map/ppermute | solution.py:21
  67.4 42.5 %collective-permute-done.2 = f32[2,64,2048]{2,1,0:T(8,128)S(1)} collective-permute-done((f32[2,64,2048]{2,1,0:T(8,128)S(1)}, f32[2,64,2048]{2,1,0:T(8,128)S(1)}, u32[]{:S(2)}, u32[]{:S(2)}) %collective-permute-start.2) | collective-permute-done | bytes 1048608 | tf_op jit(solution)/shard_map/ppermute | solution.py:21
  112.5 23.9 %collective-permute-done.3 = f32[2,64,2048]{2,1,0:T(8,128)S(1)} collective-permute-done((f32[2,64,2048]{2,1,0:T(8,128)S(1)}, f32[2,64,2048]{2,1,0:T(8,128)S(1)}, u32[]{:S(2)}, u32[]{:S(2)}) %collective-permute-start.3) | collective-permute-done | bytes 1048608 | tf_op jit(solution)/shard_map/ppermute | solution.py:21
  136.9 4.6 collective-permute-start.4
  144.1 19.5 %collective-permute-done.4 = f32[2,64,2048]{2,1,0:T(8,128)S(1)} collective-permute-done((f32[2,64,2048]{2,1,0:T(8,128)S(1)}, f32[2,64,2048]{2,1,0:T(8,128)S(1)}, u32[]{:S(2)}, u32[]{:S(2)}) %collective-permute-start.4) | collective-permute-done | bytes 1048608 | tf_op jit(solution)/shard_map/ppermute | solution.py:21
  170.5 17.8 %collective-permute-done.5 = f32[2,64,2048]{2,1,0:T(8,128)S(1)} collective-permute-done((f32[2,64,2048]{2,1,0:T(8,128)S(1)}, f32[2,64,2048]{2,1,0:T(8,128)S(1)}, u32[]{:S(2)}, u32[]{:S(2)}) %collective-permute-start.5) | collective-permute-done | bytes 1048608 | tf_op jit(solution)/shard_map/ppermute | solution.py:21
  199.2 19.9 %collective-permute-done.6 = f32[2,64,2048]{2,1,0:T(8,128)S(1)} collective-permute-done((f32[2,64,2048]{2,1,0:T(8,128)S(1)}, f32[2,64,2048]{2,1,0:T(8,128)S(1)}, u32[]{:S(2)}, u32[]{:S(2)}) %collective-permute-start.6) | collective-permute-done | bytes 1048608 | tf_op jit(solution)/shard_map/ppermute | solution.py:21
  219.5 4.8 collective-permute-start.7
  224.4 19.0 %collective-permute-done.7 = f32[2,64,2048]{2,1,0:T(8,128)S(1)} collective-permute-done((f32[2,64,2048]{2,1,0:T(8,128)S(1)}, f32[2,64,2048]{2,1,0:T(8,128)S(1)}, u32[]{:S(2)}, u32[]{:S(2)}) %collective-permute-start.7) | collective-permute-done | bytes 1048608 | tf_op jit(solution)/shard_map/ppermute | solution.py:21
  243.8 3.5 collective-permute-start.8
  247.5 18.1 %collective-permute-done.8 = f32[2,64,2048]{2,1,0:T(8,128)S(1)} collective-permute-done((f32[2,64,2048]{2,1,0:T(8,128)S(1)}, f32[2,64,2048]{2,1,0:T(8,128)S(1)}, u32[]{:S(2)}, u32[]{:S(2)}) %collective-permute-start.8) | collective-permute-done | bytes 1048608 | tf_op jit(solution)/shard_map/ppermute | solution.py:21
  266.1 6.4 %collective-permute-start.9 = (f32[2,64,2048]{2,1,0:T(8,128)S(1)}, f32[2,64,2048]{2,1,0:T(8,128)S(1)}, u32[]{:S(2)}, u32[]{:S(2)}) collective-permute-start(f32[2,64,2048]{2,1,0:T(8,128)S(1)} %pad_maximum_fusion.7), channel_id=1, source_target_pairs={{0,128},{16,144},{32,160},{48,176},{64,192},{80,208},{96,224},{112... | collective-permute-start | bytes 3145736 | tf_op jit(solution)/shard_map/ppermute | solution.py:21
  272.7 44.7 %collective-permute-done.9 = f32[2,64,2048]{2,1,0:T(8,128)S(1)} collective-permute-done((f32[2,64,2048]{2,1,0:T(8,128)S(1)}, f32[2,64,2048]{2,1,0:T(8,128)S(1)}, u32[]{:S(2)}, u32[]{:S(2)}) %collective-permute-start.9) | collective-permute-done | bytes 1048608 | tf_op jit(solution)/shard_map/ppermute | solution.py:21
  317.8 5.2 %collective-permute-start.10 = (f32[2,64,2048]{2,1,0:T(8,128)S(1)}, f32[2,64,2048]{2,1,0:T(8,128)S(1)}, u32[]{:S(2)}, u32[]{:S(2)}) collective-permute-start(f32[2,64,2048]{2,1,0:T(8,128)S(1)} %pad_maximum_fusion.8), channel_id=1, source_target_pairs={{0,256},{16,272},{32,288},{48,304},{64,320},{80,336},{96,352},{112... | collective-permute-start | bytes 3145736 | tf_op jit(solution)/shard_map/ppermute | solution.py:21
  324.5 46.5 %collective-permute-done.10 = f32[2,64,2048]{2,1,0:T(8,128)S(1)} collective-permute-done((f32[2,64,2048]{2,1,0:T(8,128)S(1)}, f32[2,64,2048]{2,1,0:T(8,128)S(1)}, u32[]{:S(2)}, u32[]{:S(2)}) %collective-permute-start.10) | collective-permute-done | bytes 1048608 | tf_op jit(solution)/shard_map/ppermute | solution.py:21
  376.0 6.6 %collective-permute-done.11 = f32[64,2048]{1,0:T(8,128)S(1)} collective-permute-done((f32[64,2048]{1,0:T(8,128)S(1)}, f32[64,2048]{1,0:T(8,128)S(1)}, u32[]{:S(2)}, u32[]{:S(2)}) %collective-permute-start.11) | collective-permute-done | bytes 524320 | tf_op jit(solution)/shard_map/ppermute | solution.py:17
  398.9 22.7 %all-gather = f32[32,1,2048]{2,1,0:T(1,128)S(1)} all-gather(f32[2,1,2048]{2,1,0:T(1,128)S(1)} %slice_add_fusion.4), channel_id=2, replica_groups=mesh['fiber'=32,'tm'=16] {'tm'}, dimensions={0}, use_global_device_ids=true | all-gather | bytes 278528 | tf_op jit(solution)/shard_map/all_gather | solution.py:26
  424.8 15.6 %all-gather.1 = f32[32,1,2048]{2,1,0:T(1,128)S(1)} all-gather(f32[2,1,2048]{2,1,0:T(1,128)S(1)} %slice_add_fusion.1), channel_id=3, replica_groups=mesh['fiber'=32,'tm'=16] {'tm'}, dimensions={0}, use_global_device_ids=true | all-gather | bytes 278528 | tf_op jit(solution)/shard_map/all_gather | solution.py:26
  442.8 12.5 %while.32 = (s32[]{:T(128)}, f32[2,2048]{1,0:T(2,128)S(1)}, f32[2,2048]{1,0:T(2,128)S(1)}, s32[]{:T(128)}, f32[16,2,2048]{2,1,0:T(2,128)}, /*index=5*/f32[16,2,2048]{2,1,0:T(2,128)S(1)}, s32[]{:T(128)}, s32[]{:T(128)}) while((s32[]{:T(128)}, f32[2,2048]{1,0:T(2,128)S(1)}, f32[2,2048]{1,0:T(2,128)S(1)}, s32[]{:T(128)}, ...), condition=%wide.region_1.2_spmd.clone, body=%wide.region_0.1_spmd.clone.sunk | while | flops 28676 | bytes 98421 | solution.py:38
  458.8 16.8 %all-gather.2 = f32[16,1,2048]{2,1,0:T(1,128)S(1)} all-gather(f32[1,1,2048]{2,1,0:T(1,128)S(1)} %slice_bitcast_fusion.4), channel_id=1, replica_groups=mesh['fiber'=32,'tm'=16] {'tm'}, dimensions={0}, use_global_device_ids=true | all-gather | bytes 139264 | tf_op jit(solution)/shard_map/all_gather | solution.py:26
  475.7 14.8 %all-gather.3 = f32[16,1,2048]{2,1,0:T(1,128)S(1)} all-gather(f32[1,1,2048]{2,1,0:T(1,128)S(1)} %slice_bitcast_fusion.3), channel_id=1, replica_groups=mesh['fiber'=32,'tm'=16] {'tm'}, dimensions={0}, use_global_device_ids=true | all-gather | bytes 139264 | tf_op jit(solution)/shard_map/all_gather | solution.py:26
  (249 shorter events, 75.5 us)
Async XLA Ops:
  0.6 9.4 %collective-permute-start = (bf16[64,2048]{1,0:T(8,128)(2,1)}, bf16[64,2048]{1,0:T(8,128)(2,1)S(1)}, u32[]{:S(2)}, u32[]{:S(2)}) collective-permute-start(bf16[64,2048]{1,0:T(8,128)(2,1)} %param.10), channel_id=1, source_target_pairs={{0,1},{1,2},{2,3},{3,4},{4,5},{5,6},{6,7},{7,8},{8,9},{9,10},{10,1... | collective-permute-start | bytes 786440 | tf_op jit(solution)/shard_map/ppermute | solution.py:17
  12.2 52.8 %collective-permute-start.1 = (f32[2,64,2048]{2,1,0:T(8,128)S(1)}, f32[2,64,2048]{2,1,0:T(8,128)S(1)}, u32[]{:S(2)}, u32[]{:S(2)}) collective-permute-start(f32[2,64,2048]{2,1,0:T(8,128)S(1)} %fusion.3), channel_id=1, source_target_pairs={{0,256},{16,272},{32,288},{48,304},{64,320},{80,336},{96,352},{112... | collective-permute-start | bytes 3145736 | tf_op jit(solution)/shard_map/ppermute | solution.py:21
  65.4 44.6 %collective-permute-start.2 = (f32[2,64,2048]{2,1,0:T(8,128)S(1)}, f32[2,64,2048]{2,1,0:T(8,128)S(1)}, u32[]{:S(2)}, u32[]{:S(2)}) collective-permute-start(f32[2,64,2048]{2,1,0:T(8,128)S(1)} %pad_maximum_fusion), channel_id=1, source_target_pairs={{0,128},{16,144},{32,160},{48,176},{64,192},{80,208},{96,224},{112... | collective-permute-start | bytes 3145736 | tf_op jit(solution)/shard_map/ppermute | solution.py:21
  110.3 26.1 %collective-permute-start.3 = (f32[2,64,2048]{2,1,0:T(8,128)S(1)}, f32[2,64,2048]{2,1,0:T(8,128)S(1)}, u32[]{:S(2)}, u32[]{:S(2)}) collective-permute-start(f32[2,64,2048]{2,1,0:T(8,128)S(1)} %pad_maximum_fusion.1), channel_id=1, source_target_pairs={{0,64},{16,80},{32,96},{48,112},{64,0},{80,16},{96,32},{112,48},{1... | collective-permute-start | bytes 3145736 | tf_op jit(solution)/shard_map/ppermute | solution.py:21
  136.9 26.7 %collective-permute-start.4 = (f32[2,64,2048]{2,1,0:T(8,128)S(1)}, f32[2,64,2048]{2,1,0:T(8,128)S(1)}, u32[]{:S(2)}, u32[]{:S(2)}) collective-permute-start(f32[2,64,2048]{2,1,0:T(8,128)S(1)} %pad_maximum_fusion.2), channel_id=1, source_target_pairs={{0,32},{16,48},{32,0},{48,16},{64,96},{80,112},{96,64},{112,80},{1... | collective-permute-start | bytes 3145736 | tf_op jit(solution)/shard_map/ppermute | solution.py:21
  164.0 24.3 %collective-permute-start.5 = (f32[2,64,2048]{2,1,0:T(8,128)S(1)}, f32[2,64,2048]{2,1,0:T(8,128)S(1)}, u32[]{:S(2)}, u32[]{:S(2)}) collective-permute-start(f32[2,64,2048]{2,1,0:T(8,128)S(1)} %pad_maximum_fusion.3), channel_id=1, source_target_pairs={{0,16},{16,0},{32,48},{48,32},{64,80},{80,64},{96,112},{112,96},{1... | collective-permute-start | bytes 3145736 | tf_op jit(solution)/shard_map/ppermute | solution.py:21
  195.7 23.4 %collective-permute-start.6 = (f32[2,64,2048]{2,1,0:T(8,128)S(1)}, f32[2,64,2048]{2,1,0:T(8,128)S(1)}, u32[]{:S(2)}, u32[]{:S(2)}) collective-permute-start(f32[2,64,2048]{2,1,0:T(8,128)S(1)} %pad_maximum_fusion.4), channel_id=1, source_target_pairs={{0,16},{16,0},{32,48},{48,32},{64,80},{80,64},{96,112},{112,96},{1... | collective-permute-start | bytes 3145736 | tf_op jit(solution)/shard_map/ppermute | solution.py:21
  219.5 24.0 %collective-permute-start.7 = (f32[2,64,2048]{2,1,0:T(8,128)S(1)}, f32[2,64,2048]{2,1,0:T(8,128)S(1)}, u32[]{:S(2)}, u32[]{:S(2)}) collective-permute-start(f32[2,64,2048]{2,1,0:T(8,128)S(1)} %pad_maximum_fusion.5), channel_id=1, source_target_pairs={{0,32},{16,48},{32,0},{48,16},{64,96},{80,112},{96,64},{112,80},{1... | collective-permute-start | bytes 3145736 | tf_op jit(solution)/shard_map/ppermute | solution.py:21
  243.8 21.8 %collective-permute-start.8 = (f32[2,64,2048]{2,1,0:T(8,128)S(1)}, f32[2,64,2048]{2,1,0:T(8,128)S(1)}, u32[]{:S(2)}, u32[]{:S(2)}) collective-permute-start(f32[2,64,2048]{2,1,0:T(8,128)S(1)} %pad_maximum_fusion.6), channel_id=1, source_target_pairs={{0,64},{16,80},{32,96},{48,112},{64,0},{80,16},{96,32},{112,48},{1... | collective-permute-start | bytes 3145736 | tf_op jit(solution)/shard_map/ppermute | solution.py:21
  266.0 6.7 %copy-start.8 = (s32[2048]{0:T(1024)S(1)}, s32[2048]{0:T(1024)}, u32[]{:S(2)}) copy-start(s32[2048]{0:T(1024)} %param.12) | copy-start | bytes 24580
  266.1 6.6 %copy-start.7 = (s32[2048]{0:T(1024)S(1)}, s32[2048]{0:T(1024)}, u32[]{:S(2)}) copy-start(s32[2048]{0:T(1024)} %param.13) | copy-start | bytes 24580
  266.1 51.3 %collective-permute-start.9 = (f32[2,64,2048]{2,1,0:T(8,128)S(1)}, f32[2,64,2048]{2,1,0:T(8,128)S(1)}, u32[]{:S(2)}, u32[]{:S(2)}) collective-permute-start(f32[2,64,2048]{2,1,0:T(8,128)S(1)} %pad_maximum_fusion.7), channel_id=1, source_target_pairs={{0,128},{16,144},{32,160},{48,176},{64,192},{80,208},{96,224},{112... | collective-permute-start | bytes 3145736 | tf_op jit(solution)/shard_map/ppermute | solution.py:21
  317.8 53.2 %collective-permute-start.10 = (f32[2,64,2048]{2,1,0:T(8,128)S(1)}, f32[2,64,2048]{2,1,0:T(8,128)S(1)}, u32[]{:S(2)}, u32[]{:S(2)}) collective-permute-start(f32[2,64,2048]{2,1,0:T(8,128)S(1)} %pad_maximum_fusion.8), channel_id=1, source_target_pairs={{0,256},{16,272},{32,288},{48,304},{64,320},{80,336},{96,352},{112... | collective-permute-start | bytes 3145736 | tf_op jit(solution)/shard_map/ppermute | solution.py:21
  372.1 2.6 copy-start.9
  372.1 3.3 copy-start.10
  372.2 10.5 %collective-permute-start.11 = (f32[64,2048]{1,0:T(8,128)S(1)}, f32[64,2048]{1,0:T(8,128)S(1)}, u32[]{:S(2)}, u32[]{:S(2)}) collective-permute-start(f32[64,2048]{1,0:T(8,128)S(1)} %slice_bitcast_fusion), channel_id=1, source_target_pairs={{1,0},{2,1},{3,2},{4,3},{5,4},{6,5},{7,6},{8,7},{9,8},{10,9},{11,1... | collective-permute-start | bytes 1572872 | tf_op jit(solution)/shard_map/ppermute | solution.py:17
  384.7 1.2 copy-start.2
  384.9 0.7 copy-start.4
  386.9 0.7 copy-start.3
  387.7 0.7 slice-start
  391.9 1.0 copy-start.1
  456.9 0.7 copy-start.6
  457.6 0.8 copy-start
  491.6 0.7 copy-start.5
  (1 other events, 0.7 us)
where the time goes:
time: 496 us; the launch traced here: 493 us
  waiting for transfers between devices  308 us (62%)
  blocking collectives  69.9 us (14%)
  starting transfers between devices  50.1 us (10%)
  other arithmetic  36.2 us (7%)
  local copies, waits for them, and re-layouts  16.7 us (3%)
  matrix products  8.29 us (2%)
    ppermute x10, waiting for transfers between devices, partner_2(): lax.ppermute(array, axis, [(i, i ^ 1 << apart) for i in range(lax.axis_si...  297 us
    all_gather x4, blocking collectives, entering(): everything = jax.tree.map(lambda part: lax.all_gather(part, axis), array)  69.9 us
    ppermute x10, starting transfers between devices, partner_2(): lax.ppermute(array, axis, [(i, i ^ 1 << apart) for i in range(lax.axis_si...  42.2 us
    select_n x32, other arithmetic, lap(): return jax.tree.map(lambda a, b: jnp.where(reached, a, b), new, before)  12.3 us
    ppermute x2, waiting for transfers between devices, passed_along(): return lax.ppermute(block, axis, route)  10.4 us
  transfers between devices with their start and end apart: 12, of which 12 were waited for; matrix products, arithmetic and copies ran while one was open for 2% of the time, Pallas kernels for 0%

commit v1 on v0

v1 whole, which is shorter than its diff:
```python
import functools
import math

import jax
import jax.numpy as jnp
import numpy as np
from jax import lax
from jax.experimental import pallas as pl
from jax.experimental.pallas import tpu as pltpu
from jax.sharding import PartitionSpec as P

FRAME = 128
HOP = 64
BINS = 64
LANES = 128
ROWS = 16
BLOCK = 128
TOP = 32512.0
MESH = pl.DeviceIdType.MESH
F32 = jnp.float32
BF16 = jnp.bfloat16


def halves(table):
    high = table.astype(np.float32).astype(jnp.bfloat16)
    low = (table - high.astype(np.float64)).astype(np.float32).astype(jnp.bfloat16)
    return high, low


def time_order():
    rows = np.arange(HOP)
    return 8 * (rows % 8) + rows // 8


def tables(total):
    rows = total // LANES
    n = np.arange(FRAME)
    f = np.arange(BINS)
    angle = 2.0 * math.pi / FRAME * ((f[:, None] * n[None, :]) % FRAME)
    window = 0.5 - 0.5 * np.cos(2.0 * math.pi / FRAME * n)
    analysis = np.concatenate([window * np.cos(angle), -window * np.sin(angle)], 0)
    weight = np.where(f == 0, 1.0, 2.0)[:, None] / FRAME
    synthesis = np.concatenate([weight * np.cos(angle), -weight * np.sin(angle)], 0).T
    order = time_order()
    synthesis = synthesis[np.concatenate([order, HOP + order])]
    a = np.arange(rows)
    outer = 2.0 * math.pi / rows * ((a[:, None] * a[None, :]) % rows)
    blocks = rows // BLOCK
    outer = np.stack(
        [np.cos(outer).reshape(blocks, BLOCK, rows), -np.sin(outer).reshape(blocks, BLOCK, rows)], 1
    ).reshape(blocks, 2 * BLOCK, rows)
    b = np.arange(LANES)
    turn = 2.0 * math.pi / total * ((a[:, None] * b[None, :]) % total)
    turn = np.concatenate([np.cos(turn), -np.sin(turn)], 1)
    inner = 2.0 * math.pi / LANES * ((b[:, None] * b[None, :]) % LANES)
    cos, sin = np.cos(inner), np.sin(inner)
    forward = np.block([[cos, -sin], [sin, cos]])
    inverse = np.block([[cos, sin], [-sin, cos]]) / total
    ah, al = halves(analysis)
    sh, sl = halves(synthesis)
    oh, ol = halves(outer)
    fh, fl = halves(forward)
    ih, il = halves(inverse)
    return (
        np.concatenate([ah, al], 0),
        np.concatenate([sh, sh, sl], 1),
        np.concatenate([oh, oh, ol], 2),
        turn.astype(np.float32),
        np.concatenate([fh, fh, fl], 0),
        np.concatenate([ih, ih, il], 0),
    )


def split(x):
    high = x.astype(BF16)
    return high, (x - high.astype(F32)).astype(BF16)


def across(x):
    high, low = split(x)
    return jnp.concatenate([high, low, high], axis=1)


def peak_of(x):
    top = jnp.max(jnp.max(jnp.abs(x), axis=0, keepdims=True), axis=1, keepdims=True)
    return jnp.maximum(top, 1e-30)


def coded(x, gain):
    return jnp.round(x * gain).astype(jnp.int32).astype(jnp.int16)


def kernel(
    nf,
    nt,
    strain,
    cut,
    sta,
    lta,
    drift,
    limit,
    ana,
    syn,
    outer,
    turn,
    fwd,
    inv,
    filtered,
    ratio,
    ph,
    rim,
    spec,
    snd1,
    rcv1,
    scs1,
    scr1,
    x3,
    z3,
    snd2,
    rcv2,
    scs2,
    scr2,
    deco,
    head,
    tail,
    sps,
    spr,
    sss,
    ssr,
    lev,
    seg,
    cars,
    carr,
    sums,
    sumr,
    temp,
    rim_sem,
    s1s,
    s1r,
    c1s,
    c1r,
    s2s,
    s2r,
    c2s,
    c2r,
    sp_s,
    sp_r,
    ss_s,
    ss_r,
    ca_s,
    ca_r,
    su_s,
    su_r,
):
    me = lax.axis_index("fiber")
    tm = lax.axis_index("tm")
    per = BINS // nf
    rows = nf * ROWS
    blocks = rows // BLOCK
    total = rows * LANES
    chans = ROWS * LANES
    later, earlier = lax.rem(tm + 1, nt), lax.rem(tm + nt - 1, nt)

    def remote(src, dst, send, recv, **to):
        return pltpu.make_async_remote_copy(
            src_ref=src, dst_ref=dst, send_sem=send, recv_sem=recv, device_id=to, device_id_type=MESH
        )

    barrier = pltpu.get_barrier_semaphore()

    def greet_fiber(j, c):
        pl.semaphore_signal(
            barrier, inc=1, device_id={"fiber": lax.rem(me + j, nf)}, device_id_type=MESH
        )
        return c

    def greet_tm(j, c):
        pl.semaphore_signal(
            barrier, inc=1, device_id={"tm": lax.rem(tm + j, nt)}, device_id_type=MESH
        )
        return c

    lax.fori_loop(1, nf, greet_fiber, 0)
    lax.fori_loop(1, nt, greet_tm, 0)
    pl.semaphore_wait(barrier, nf - 1 + nt - 1)

    rim_copy = remote(strain, rim, rim_sem.at[0], rim_sem.at[1], tm=later)
    rim_copy.start()
    rim_copy.wait()
    has_rim = jnp.where(tm > 0, 1.0, 0.0).astype(F32)

    peak = jnp.zeros((1, 1), F32)
    for q in range(0, ROWS, 2):
        cols = slice(q * LANES, (q + 2) * LANES)
        before = (rim[:, cols].astype(F32) * has_rim).astype(BF16)
        frame = jnp.concatenate([before, strain[:, cols]], axis=0)
        both = jnp.dot(ana[...], frame, preferred_element_type=F32)
        got = both[:FRAME] + both[FRAME:]
        spec[:, q, :] = got[:, :LANES]
        spec[:, q + 1, :] = got[:, LANES:]
        peak = jnp.maximum(peak, peak_of(got))
    gain = TOP / peak
    scs1[0] = jnp.broadcast_to(peak * (1.0 / TOP), (1, LANES))
    scr1[me] = scs1[0]

    def code1(f):
        snd1[f, :, 0:LANES] = coded(spec[f], gain)
        snd1[f, :, LANES : 2 * LANES] = coded(spec[BINS + f], gain)

    def scale1(j):
        to = lax.rem(me + j, nf)
        return remote(scs1.at[0], scr1.at[me], c1s.at[j], c1r.at[j], fiber=to)

    def data1(b, j):
        to = lax.rem(me + j, nf)
        return remote(
            snd1.at[to * per + b],
            rcv1.at[b, pl.ds(pl.multiple_of(me * ROWS, ROWS), ROWS), :],
            s1s.at[b, j],
            s1r.at[b, j],
            fiber=to,
        )

    def from1(b, j):
        back = lax.rem(me + nf - j, nf)
        return remote(
            snd1.at[0],
            rcv1.at[b, pl.ds(pl.multiple_of(back * ROWS, ROWS), ROWS), :],
            s1s.at[b, j],
            s1r.at[b, j],
            fiber=back,
        )

    def out_scale(j, c):
        scale1(j).start()
        return c

    lax.fori_loop(1, nf, out_scale, 0)

    def out_bins(b, c):
        def out_peer(j, c):
            code1(lax.rem(me + j, nf) * per + b)
            data1(b, j).start()
            return c

        lax.fori_loop(1, nf, out_peer, 0)
        code1(me * per + b)
        rcv1[b, pl.ds(pl.multiple_of(me * ROWS, ROWS), ROWS), :] = snd1[me * per + b]
        return c

    lax.fori_loop(0, per, out_bins, 0)

    def in_scale(j, c):
        back = lax.rem(me + nf - j, nf)
        remote(scs1.at[0], scr1.at[back], c1s.at[j], c1r.at[j], fiber=back).wait_recv()
        return c

    lax.fori_loop(1, nf, in_scale, 0)

    peers = BLOCK // ROWS

    def scale2(b, blk, to):
        j = lax.rem(to - me + nf, nf)
        return remote(
            scs2.at[b, blk], scr2.at[me * per + b], c2s.at[b, j], c2r.at[b, j], fiber=to
        )

    def data2(b, to):
        j = lax.rem(to - me + nf, nf)
        return remote(
            snd2.at[b, pl.ds(pl.multiple_of(to * ROWS, ROWS), ROWS), :],
            rcv2.at[me * per + b],
            s2s.at[b, j],
            s2r.at[b, j],
            fiber=to,
        )

    lane = lax.broadcasted_iota(jnp.int32, (BLOCK, LANES), 1)
    row = lax.broadcasted_iota(jnp.int32, (BLOCK, LANES), 0)

    def one_bin(b, c):
        def in_peer(j, c):
            from1(b, j).wait_recv()
            return c

        lax.fori_loop(1, nf, in_peer, 0)
        limit_k = cut[me * per + b]

        def decode(p, c):
            at = pl.multiple_of(p * ROWS, ROWS)
            scale = scr1[p]
            x = rcv1[b, pl.ds(at, ROWS), :].astype(F32)
            x = x * jnp.concatenate([scale, scale], axis=1)
            high, low = split(x)
            x3[pl.ds(at, ROWS), :] = high
            x3[pl.ds(pl.multiple_of(rows + at, ROWS), ROWS), :] = low
            x3[pl.ds(pl.multiple_of(2 * rows + at, ROWS), ROWS), :] = high
            return c

        lax.fori_loop(0, nf, decode, 0)

        def to_waves(blk, c):
            at = pl.multiple_of(blk * BLOCK, BLOCK)
            pq = jnp.dot(outer[blk], x3[...], preferred_element_type=F32)
            re = pq[:BLOCK, :LANES] - pq[BLOCK:, LANES:]
            im = pq[:BLOCK, LANES:] + pq[BLOCK:, :LANES]
            tr = turn[pl.ds(at, BLOCK), 0:LANES]
            ti = turn[pl.ds(at, BLOCK), LANES : 2 * LANES]
            y = jnp.concatenate([re * tr - im * ti, re * ti + im * tr], axis=1)
            w = jnp.dot(across(y), fwd[...], preferred_element_type=F32)
            k = row + blk * BLOCK + rows * lane
            keep = jnp.minimum(k, total - k) <= limit_k
            w = jnp.concatenate(
                [jnp.where(keep, w[:, :LANES], 0.0), jnp.where(keep, w[:, LANES:], 0.0)], axis=1
            )
            z = jnp.dot(across(w), inv[...], preferred_element_type=F32)
            re, im = z[:, :LANES], z[:, LANES:]
            z = jnp.concatenate([re * tr + im * ti, im * tr - re * ti], axis=1)
            high, low = split(z)
            z3[pl.ds(at, BLOCK), :] = high
            z3[pl.ds(pl.multiple_of(rows + at, BLOCK), BLOCK), :] = low
            z3[pl.ds(pl.multiple_of(2 * rows + at, BLOCK), BLOCK), :] = high
            return c

        lax.fori_loop(0, blocks, to_waves, 0)

        def to_channels(blk, c):
            at = pl.multiple_of(blk * BLOCK, BLOCK)
            pq = jnp.dot(outer[blk], z3[...], preferred_element_type=F32)
            re = pq[:BLOCK, :LANES] + pq[BLOCK:, LANES:]
            im = pq[:BLOCK, LANES:] - pq[BLOCK:, :LANES]
            x = jnp.concatenate([re, im], axis=1)
            top = peak_of(x)
            scs2[b, blk] = jnp.broadcast_to(top * (1.0 / TOP), (1, LANES))
            snd2[b, pl.ds(at, BLOCK), :] = coded(x, TOP / top)

            def out_peer(i, c):
                to = blk * peers + i

                @pl.when(to != me)
                def _():
                    scale2(b, blk, to).start()
                    data2(b, to).start()

                @pl.when(to == me)
                def _():
                    scr2[me * per + b] = scs2[b, blk]
                    mine = pl.multiple_of(me * ROWS, ROWS)
                    rcv2[me * per + b] = snd2[b, pl.ds(mine, ROWS), :]

                return c

            lax.fori_loop(0, peers, out_peer, 0)
            return c

        lax.fori_loop(0, blocks, to_channels, 0)
        return c

    lax.fori_loop(0, per, one_bin, 0)

    def in_back(j, c):
        back = lax.rem(me + nf - j, nf)

        def in_bin(b, c):
            f = back * per + b
            remote(scs2.at[0, 0], scr2.at[f], c2s.at[b, j], c2r.at[b, j], fiber=back).wait_recv()
            remote(
                snd2.at[0, pl.ds(0, ROWS), :], rcv2.at[f], s2s.at[b, j], s2r.at[b, j], fiber=back
            ).wait_recv()
            return c

        lax.fori_loop(0, per, in_bin, 0)
        return c

    lax.fori_loop(1, nf, in_back, 0)

    def decode2(f, c):
        x = rcv2[f].astype(F32)
        scale = scr2[f]
        deco[0, f] = x[:, :LANES] * scale
        deco[1, f] = x[:, LANES:] * scale
        return c

    lax.fori_loop(0, BINS, decode2, 0)

    chunks = 4
    wide = ROWS // chunks

    def spill(c):
        span = pl.ds(c * wide, wide)
        return remote(sps.at[span], spr.at[span], sp_s.at[c], sp_r.at[c], tm=earlier)

    def spill_scale(c):
        return remote(sss.at[c], ssr.at[c], ss_s.at[c], ss_r.at[c], tm=earlier)

    for chunk in range(chunks):
        top = jnp.full((1, 1), 1e-30, F32)
        for q in range(chunk * wide, (chunk + 1) * wide, 2):
            x = jnp.concatenate(
                [
                    jnp.concatenate([deco[0, :, q, :], deco[1, :, q, :]], axis=0),
                    jnp.concatenate([deco[0, :, q + 1, :], deco[1, :, q + 1, :]], axis=0),
                ],
                axis=1,
            )
            high, low = split(x)
            got = jnp.dot(
                syn[...], jnp.concatenate([high, low, high], axis=0), preferred_element_type=F32
            )
            for i in range(2):
                head[q + i] = got[:HOP, i * LANES : (i + 1) * LANES]
                tail[q + i] = got[HOP:, i * LANES : (i + 1) * LANES]
            top = jnp.maximum(top, peak_of(got[:HOP]))
        sss[chunk] = jnp.broadcast_to(top * (1.0 / TOP), (1, LANES))
        spill_scale(chunk).start()
        for q in range(chunk * wide, (chunk + 1) * wide):
            sps[q] = coded(head[q], TOP / top)
        spill(chunk).start()

    has_next = jnp.where(tm < nt - 1, 1.0, 0.0).astype(F32)
    seg_id = lax.broadcasted_iota(jnp.int32, (8, LANES), 0)

    def shifted(x, by, fill):
        return jnp.where(seg_id >= by, pltpu.roll(x, by, 0), fill)

    def rate_of(length):
        return 1.0 - 1.0 / length

    def natural(vectors):
        for i in range(8):
            temp[pl.ds(i, 8, stride=8), :] = vectors[i]
        return temp[...]

    for chunk in range(chunks):
        spill_scale(chunk).wait_recv()
        spill(chunk).wait_recv()

        def scan_row(q, c):
            at = pl.ds(q, 1)
            cols = pl.ds(pl.multiple_of(q * LANES, LANES), LANES)
            heads = spr[q].astype(F32) * (ssr[chunk] * has_next)
            rounded = (tail[q] + heads).astype(BF16).astype(F32)
            part = [rounded[8 * i : 8 * i + 8] for i in range(8)]
            filtered[:, cols] = natural(part).astype(BF16)
            energy = [v * v for v in part]
            for s, ref in enumerate((sta, lta)):
                keep = jnp.broadcast_to(rate_of(ref[at, :]), (8, LANES))
                gain = 1.0 - keep
                level = gain * energy[0]
                lev[s, q, 0:8] = level
                for i in range(1, 8):
                    level = keep * level + gain * energy[i]
                    lev[s, q, 8 * i : 8 * i + 8] = level
                power = keep * keep
                power = power * power
                power = power * power
                for by in (1, 2, 4):
                    level = level + power * shifted(level, by, 0.0)
                    power = power * power
                seg[s, q] = shifted(level, 1, 0.0)
                cars[s, at, :] = level[7:8]
            return c

        lax.fori_loop(chunk * wide, (chunk + 1) * wide, scan_row, 0)

    def to_later(snd, rcv, send, recv, j):
        return remote(snd, rcv.at[tm], send.at[j], recv.at[j], tm=lax.rem(tm + j, nt))

    def from_earlier(snd, rcv, send, recv, j):
        back = lax.rem(tm + nt - j, nt)
        return remote(snd, rcv.at[back], send.at[j], recv.at[j], tm=back)

    def pass_on(snd, rcv, send, recv):
        def out(j, c):
            to_later(snd, rcv, send, recv, j).start()
            return c

        lax.fori_loop(1, nt - tm, out, 0)

        def come(j, c):
            from_earlier(snd, rcv, send, recv, j).wait_recv()
            return c

        lax.fori_loop(1, tm + 1, come, 0)

    pass_on(cars, carr, ca_s, ca_r)
    decay = []
    for ref in (sta, lta):
        power = rate_of(ref[...])
        for _ in range(6):
            power = power * power
        decay.append(power)

    def lap(k, state):
        return tuple(decay[s] * state[s] + carr[k, s] for s in range(2))

    ones = jnp.ones((ROWS, LANES), F32)
    start = lax.fori_loop(0, tm, lap, (ones, ones))
    head[0, 0:ROWS] = start[0]
    head[1, 0:ROWS] = start[1]

    def climb_row(q, c):
        at = pl.ds(q, 1)
        cols = pl.ds(pl.multiple_of(q * LANES, LANES), LANES)
        avg = []
        for s, ref in enumerate((sta, lta)):
            keep = jnp.broadcast_to(rate_of(ref[at, :]), (8, LANES))
            carry = jnp.broadcast_to(head[s, at, :], (8, LANES))
            power = keep * keep
            power = power * power
            power = power * power
            for bit in (1, 2, 4):
                carry = jnp.where((seg_id // bit) % 2 == 1, carry * power, carry)
                power = power * power
            entry = seg[s, q] + carry
            values = []
            for i in range(8):
                entry = entry * keep
                values.append(lev[s, q, 8 * i : 8 * i + 8] + entry)
            avg.append(values)
        quotient = [avg[0][i] / avg[1][i] for i in range(8)]
        ratio[:, cols] = natural(quotient)
        rate = jnp.broadcast_to(0.5 + drift[at, :] * (1.0 / 64.0), (8, LANES))
        climb = quotient[0] - rate
        low = climb
        climbs, lows = [climb], [low]
        for i in range(1, 8):
            climb = climb + (quotient[i] - rate)
            low = jnp.minimum(low, climb)
            climbs.append(climb)
            lows.append(low)
        whole = climb
        for by in (1, 2, 4):
            whole = whole + shifted(whole, by, 0.0)
        base = shifted(whole, 1, 0.0)
        least = base + low
        for by in (1, 2, 4):
            least = jnp.minimum(least, shifted(least, by, jnp.inf))
        floor = shifted(least, 1, jnp.inf)
        for i in range(8):
            up = base + climbs[i]
            lev[0, q, 8 * i : 8 * i + 8] = up
            lev[1, q, 8 * i : 8 * i + 8] = jnp.minimum(floor, base + lows[i])
        sums[0, at, :] = whole[7:8]
        sums[1, at, :] = least[7:8]
        return c

    lax.fori_loop(0, ROWS, climb_row, 0)

    pass_on(sums, sumr, su_s, su_r)

    def lap2(k, state):
        total_up, low = state
        return total_up + sumr[k, 0], jnp.minimum(low, total_up + sumr[k, 1])

    zeros = jnp.zeros((ROWS, LANES), F32)
    before, low = lax.fori_loop(0, tm, lap2, (zeros, zeros))
    head[2, 0:ROWS] = before
    head[3, 0:ROWS] = low

    def ph_row(q, c):
        at = pl.ds(q, 1)
        cols = pl.ds(pl.multiple_of(q * LANES, LANES), LANES)
        base = jnp.broadcast_to(head[2, at, :], (8, LANES))
        low = jnp.broadcast_to(head[3, at, :], (8, LANES))
        scale = jnp.broadcast_to(1.0 / limit[at, :], (8, LANES))
        out = []
        for i in range(8):
            climb = base + lev[0, q, 8 * i : 8 * i + 8]
            lowest = jnp.minimum(low, base + lev[1, q, 8 * i : 8 * i + 8])
            out.append((climb - lowest) * scale)
        ph[:, cols] = natural(out)
        return c

    lax.fori_loop(0, ROWS, ph_row, 0)


    def sent1(j, c):
        scale1(j).wait_send()

        def sent_bin(b, c):
            data1(b, j).wait_send()
            to = lax.rem(me + j, nf)
            scale2(b, 0, to).wait_send()
            data2(b, to).wait_send()
            return c

        lax.fori_loop(0, per, sent_bin, 0)
        return c

    lax.fori_loop(1, nf, sent1, 0)
    for chunk in range(chunks):
        spill_scale(chunk).wait_send()
        spill(chunk).wait_send()

    def sent_on(j, c):
        to_later(sums, carr, ca_s, ca_r, j).wait_send()
        to_later(sums, sumr, su_s, su_r, j).wait_send()
        return c

    lax.fori_loop(1, nt - tm, sent_on, 0)


def body(nf, nt, strain, fan_cut, sta_len, lta_len, drift_code, threshold):
    per = BINS // nf
    rows = nf * ROWS
    total = rows * LANES
    blocks = rows // BLOCK
    tabs = [jnp.asarray(t) for t in tables(total)]
    per_chan = [v.astype(F32).reshape(ROWS, LANES) for v in (sta_len, lta_len, drift_code, threshold)]
    vmem = pl.BlockSpec(memory_space=pltpu.VMEM)
    smem = pl.BlockSpec(memory_space=pltpu.SMEM)
    dma = pltpu.SemaphoreType.DMA
    i16 = jnp.int16
    chans = ROWS * LANES
    return pl.pallas_call(
        functools.partial(kernel, nf, nt),
        out_shape=(
            jax.ShapeDtypeStruct((HOP, chans), BF16),
            jax.ShapeDtypeStruct((HOP, chans), F32),
            jax.ShapeDtypeStruct((HOP, chans), F32),
        ),
        in_specs=[vmem, smem] + [vmem] * 10,
        out_specs=(vmem, vmem, vmem),
        scratch_shapes=[
            pltpu.VMEM((HOP, chans), BF16),
            pltpu.VMEM((FRAME, ROWS, LANES), F32),
            pltpu.VMEM((BINS, ROWS, 2 * LANES), i16),
            pltpu.VMEM((per, rows, 2 * LANES), i16),
            pltpu.VMEM((1, 1, LANES), F32),
            pltpu.VMEM((nf, 1, LANES), F32),
            pltpu.VMEM((3 * rows, 2 * LANES), BF16),
            pltpu.VMEM((3 * rows, 2 * LANES), BF16),
            pltpu.VMEM((per, rows, 2 * LANES), i16),
            pltpu.VMEM((BINS, ROWS, 2 * LANES), i16),
            pltpu.VMEM((per, blocks, 1, LANES), F32),
            pltpu.VMEM((BINS, 1, LANES), F32),
            pltpu.VMEM((2, BINS, ROWS, LANES), F32),
            pltpu.VMEM((ROWS, HOP, LANES), F32),
            pltpu.VMEM((ROWS, HOP, LANES), F32),
            pltpu.VMEM((ROWS, HOP, LANES), i16),
            pltpu.VMEM((ROWS, HOP, LANES), i16),
            pltpu.VMEM((4, 1, LANES), F32),
            pltpu.VMEM((4, 1, LANES), F32),
            pltpu.VMEM((2, ROWS, HOP, LANES), F32),
            pltpu.VMEM((2, ROWS, 8, LANES), F32),
            pltpu.VMEM((2, ROWS, LANES), F32),
            pltpu.VMEM((nt, 2, ROWS, LANES), F32),
            pltpu.VMEM((2, ROWS, LANES), F32),
            pltpu.VMEM((nt, 2, ROWS, LANES), F32),
            pltpu.VMEM((HOP, LANES), F32),
            dma((2,)),
            dma((per, nf)),
            dma((per, nf)),
            dma((nf,)),
            dma((nf,)),
            dma((per, nf)),
            dma((per, nf)),
            dma((per, nf)),
            dma((per, nf)),
            dma((4,)),
            dma((4,)),
            dma((4,)),
            dma((4,)),
            dma((nt,)),
            dma((nt,)),
            dma((nt,)),
            dma((nt,)),
        ],
        compiler_params=pltpu.CompilerParams(
            collective_id=0, has_side_effects=True, vmem_limit_bytes=48 * 1024 * 1024
        ),
    )(strain, fan_cut, *per_chan, *tabs)


def solution(mesh):
    return jax.shard_map(
        functools.partial(body, mesh.shape["fiber"], mesh.shape["tm"]),
        mesh=mesh,
        in_specs=(P("tm", "fiber"), P(), P("fiber"), P("fiber"), P("fiber"), P("fiber")),
        out_specs=(P("tm", "fiber"), P("tm", "fiber"), P("tm", "fiber")),
        check_vma=False,
    )
```

time: 496 us -> 84.7 us (0.17)
  waiting for transfers between devices: 308 us -> 0 us
  Pallas kernels: 0 us -> 72.4 us
  blocking collectives: 69.9 us -> 0 us
  starting transfers between devices: 50.1 us -> 0 us
  other arithmetic: 36.2 us -> 1.43 us
  matrix products: 8.29 us -> 0 us
  local copies, waits for them, and re-layouts: 16.7 us -> 8.66 us
    ppermute x12 -> x0, waiting for transfers between devices: 308 us -> none  [the longest x10 297 us: partner_2(): lax.ppermute(array, axis, [(i, i ^ 1 << apart) for i in range(lax.axis_si...]
    pallas_call x0 -> x1, Pallas kernels: none -> 72.4 us  [body(): pl.pallas_call(functools.partial(kernel, nf, nt), out_shape=(jax.ShapeDty...]
    all_gather x4 -> x0, blocking collectives: 69.9 us -> none  [entering(): everything = jax.tree.map(lambda part: lax.all_gather(part, axis), array)]
    ppermute x12 -> x0, starting transfers between devices: 50.1 us -> none  [the longest x10 42.2 us: partner_2(): lax.ppermute(array, axis, [(i, i ^ 1 << apart) for i in range(lax.axis_si...]
    select_n x42 -> x0, other arithmetic: 13.8 us -> none  [the longest x32 12.3 us: lap(): return jax.tree.map(lambda a, b: jnp.where(reached, a, b), new, before)]
    dot_general x7 -> x0, matrix products: 8.29 us -> none  [the longest x1 1.86 us: local_inverse(): jnp.einsum('stbl,tqkl->sqkb', dft_block(inner_len, 1.0), grid, precision=...]
    pad x20 -> x0, local copies, waits for them, and re-layouts: 5.79 us -> none  [body(): run_gain, run_input = lax.associative_scan(affine, (gains, inputs), axis=1)]
  transfers between devices with their start and end apart: 12 -> 0, of which waited for: 12 -> 0; matrix products, arithmetic and copies ran while one was open for 2% -> 0% of each run, Pallas kernels for 0% -> 0%
where the time goes in v1:
time: 84.7 us; the launch traced here: 83.1 us
  Pallas kernels  72.4 us (85%)
  local copies, waits for them, and re-layouts  8.66 us (10%)
  other arithmetic  1.43 us (2%)
    pallas_call x1, Pallas kernels, body(): pl.pallas_call(functools.partial(kernel, nf, nt), out_shape=(jax.ShapeDty...  72.4 us
    unnamed x17, local copies, waits for them, and re-layouts  8.66 us

profile of v1, /device:TPU:1, one launch (start us, length us, event | category | flops | bytes accessed | tf_op | source)
XLA Modules:
  0.0 83.1 jit_solution(3394865671953350770)
XLA Ops:
  0.6 0.7 convert_bitcast_fusion.2
  1.3 0.7 convert_bitcast_fusion
  2.1 0.0 copy-start
  2.1 1.0 %copy-done = f32[512,256]{1,0:T(8,128)S(1)} copy-done((f32[512,256]{1,0:T(8,128)S(1)}, f32[512,256]{1,0:T(8,128)}, u32[]{:S(2)}) %copy-start) | copy-done | bytes 524312
  3.1 0.0 copy-start.1
  3.1 1.0 %copy-done.1 = bf16[768,256]{1,0:T(8,128)(2,1)S(1)} copy-done((bf16[768,256]{1,0:T(8,128)(2,1)S(1)}, bf16[768,256]{1,0:T(8,128)(2,1)}, u32[]{:S(2)}) %copy-start.1) | copy-done | bytes 393240
  4.1 0.0 copy-start.2
  4.1 1.0 %copy-done.2 = bf16[768,256]{1,0:T(8,128)(2,1)S(1)} copy-done((bf16[768,256]{1,0:T(8,128)(2,1)S(1)}, bf16[768,256]{1,0:T(8,128)(2,1)}, u32[]{:S(2)}) %copy-start.2) | copy-done | bytes 393240
  5.1 0.0 copy-start.3
  5.1 0.9 %copy-done.3 = bf16[64,2048]{1,0:T(8,128)(2,1)S(1)} copy-done((bf16[64,2048]{1,0:T(8,128)(2,1)S(1)}, bf16[64,2048]{1,0:T(8,128)(2,1)}, u32[]{:S(2)}) %copy-start.3) | copy-done | bytes 262168
  6.1 0.0 copy-start.4
  6.1 0.9 %copy-done.4 = bf16[128,384]{1,0:T(8,128)(2,1)S(1)} copy-done((bf16[128,384]{1,0:T(8,128)(2,1)S(1)}, bf16[128,384]{1,0:T(8,128)(2,1)}, u32[]{:S(2)}) %copy-start.4) | copy-done | bytes 98328
  6.9 0.0 copy-start.5
  6.9 0.8 %copy-done.5 = bf16[256,128]{1,0:T(8,128)(2,1)S(1)} copy-done((bf16[256,128]{1,0:T(8,128)(2,1)S(1)}, bf16[256,128]{1,0:T(8,128)(2,1)}, u32[]{:S(2)}) %copy-start.5) | copy-done | bytes 65560
  7.8 0.0 copy-start.6
  7.8 0.7 copy-done.6
  8.4 72.4 %shard_map.139 = (bf16[64,2048]{1,0:T(8,128)(2,1)S(1)}, f32[64,2048]{1,0:T(8,128)S(1)}, f32[64,2048]{1,0:T(8,128)S(1)}) custom-call(bf16[64,2048]{1,0:T(8,128)(2,1)S(1)} %copy-done.3, s32[64]{0:T(128)S(1)} %copy-done.6, f32[16,128]{1,0:T(8,128)S(1)} %get-tuple-element.6.sta, f32[16,128]{1,0:T(8,128)S(1)} %get-tuple-element.5.lta, ...), custom_call_target="tpu_custom_call" | custom-call | tf_op jit(solution)/shard_map/pallas_call | solution.py:616
  80.8 0.7 copy.18
  81.5 0.8 copy.19
  82.3 0.8 copy.20
Async XLA Ops:
  2.1 1.0 %copy-start = (f32[512,256]{1,0:T(8,128)S(1)}, f32[512,256]{1,0:T(8,128)}, u32[]{:S(2)}) copy-start(f32[512,256]{1,0:T(8,128)} %constant.15.clone.turn) | copy-start | bytes 1572868
  3.1 1.0 %copy-start.1 = (bf16[768,256]{1,0:T(8,128)(2,1)S(1)}, bf16[768,256]{1,0:T(8,128)(2,1)}, u32[]{:S(2)}) copy-start(bf16[768,256]{1,0:T(8,128)(2,1)} %constant.17.clone.inv) | copy-start | bytes 1179652
  4.1 1.0 %copy-start.2 = (bf16[768,256]{1,0:T(8,128)(2,1)S(1)}, bf16[768,256]{1,0:T(8,128)(2,1)}, u32[]{:S(2)}) copy-start(bf16[768,256]{1,0:T(8,128)(2,1)} %constant.16.clone.fwd) | copy-start | bytes 1179652
  5.1 0.9 %copy-start.3 = (bf16[64,2048]{1,0:T(8,128)(2,1)S(1)}, bf16[64,2048]{1,0:T(8,128)(2,1)}, u32[]{:S(2)}) copy-start(bf16[64,2048]{1,0:T(8,128)(2,1)} %strain.1) | copy-start | bytes 786436
  6.1 0.9 %copy-start.4 = (bf16[128,384]{1,0:T(8,128)(2,1)S(1)}, bf16[128,384]{1,0:T(8,128)(2,1)}, u32[]{:S(2)}) copy-start(bf16[128,384]{1,0:T(8,128)(2,1)} %constant.13.clone.syn) | copy-start | bytes 294916
  6.9 0.8 %copy-start.5 = (bf16[256,128]{1,0:T(8,128)(2,1)S(1)}, bf16[256,128]{1,0:T(8,128)(2,1)}, u32[]{:S(2)}) copy-start(bf16[256,128]{1,0:T(8,128)(2,1)} %constant.12.clone.ana) | copy-start | bytes 196612
  7.8 0.7 copy-start.6

commit v2 on v1

v2 whole, which is shorter than its diff:
```python
import functools
import math

import jax
import jax.numpy as jnp
import numpy as np
from jax import lax
from jax.experimental import pallas as pl
from jax.experimental.pallas import tpu as pltpu
from jax.sharding import PartitionSpec as P

FRAME = 128
HOP = 64
BINS = 64
LANES = 128
ROWS = 16
GROUP = 4
TOP = 32512.0
MESH = pl.DeviceIdType.MESH
F32 = jnp.float32
BF16 = jnp.bfloat16


def time_order():
    rows = np.arange(HOP)
    return 8 * (rows % 8) + rows // 8


def tables(total):
    rows = total // LANES
    half = rows // 2
    n = np.arange(FRAME)
    f = np.arange(BINS)
    angle = 2.0 * math.pi / FRAME * ((f[:, None] * n[None, :]) % FRAME)
    window = 0.5 - 0.5 * np.cos(2.0 * math.pi / FRAME * n)
    analysis = np.concatenate([window * np.cos(angle), -window * np.sin(angle)], 0)
    weight = np.where(f == 0, 1.0, 2.0)[:, None] / FRAME
    synthesis = np.concatenate([weight * np.cos(angle), -weight * np.sin(angle)], 0).T
    order = time_order()
    synthesis = synthesis[np.concatenate([order, HOP + order])]
    a = np.arange(half)
    outer = 2.0 * math.pi / half * ((a[:, None] * a[None, :]) % half)
    outer = np.concatenate([np.cos(outer), -np.sin(outer)], 0)
    step = np.broadcast_to(2.0 * math.pi / rows * a[:, None], (half, LANES))
    step = np.concatenate([np.cos(step), -np.sin(step)], 1)
    b = np.arange(LANES)
    wave = np.concatenate([2 * a, 2 * a + 1])
    turn = 2.0 * math.pi / total * ((wave[:, None] * b[None, :]) % total)
    turn = np.concatenate([np.cos(turn), -np.sin(turn)], 1)
    inner = 2.0 * math.pi / LANES * ((b[:, None] * b[None, :]) % LANES)
    cos, sin = np.cos(inner), np.sin(inner)
    forward = np.block([[cos, -sin], [sin, cos]])
    inverse = np.block([[cos, sin], [-sin, cos]]) / total
    return [t.astype(np.float32) for t in (analysis, outer, forward, inverse, synthesis, step, turn)]


def split(x):
    high = x.astype(BF16)
    return high, (x - high.astype(F32)).astype(BF16)


def across(x):
    high, low = split(x)
    return jnp.concatenate([high, low, high], axis=1)


def peak_of(x):
    top = jnp.max(jnp.max(jnp.abs(x), axis=0, keepdims=True), axis=1, keepdims=True)
    return jnp.maximum(top, 1e-30)


def coded(x, gain):
    return jnp.round(x * gain).astype(jnp.int32).astype(jnp.int16)


def kernel(
    nf,
    nt,
    *refs,
):
    (
        strain_far,
        cut_far,
        sta_far,
        lta_far,
        drift_far,
        limit_far,
        ana_far,
        outer_far,
        fwd_far,
        inv_far,
        syn_far,
        step_far,
        turn_far,
        filtered_far,
        ratio_far,
        ph_far,
        strain,
        cut,
        chan,
        ana_raw,
        outer_raw,
        fwd_raw,
        inv_raw,
        syn_raw,
        step,
        turn,
        ana,
        outer,
        fwd,
        inv,
        syn,
        filtered,
        ratio,
        ph,
        rim,
        spec,
        snd1,
        rcv1,
        scs1,
        scr1,
        x3,
        z3,
        snd2,
        rcv2,
        scs2,
        scr2,
        deco,
        head,
        tail,
        sps,
        spr,
        sss,
        ssr,
        lev,
        seg,
        cars,
        carr,
        sums,
        sumr,
        temp,
        rim_s,
        rim_r,
        s1s,
        s1r,
        c1s,
        c1r,
        s2s,
        s2r,
        c2s,
        c2r,
        sp_s,
        sp_r,
        ss_s,
        ss_r,
        ca_s,
        ca_r,
        su_s,
        su_r,
        load_sem,
        store_sem,
    ) = refs
    me = lax.axis_index("fiber")
    tm = lax.axis_index("tm")
    per = BINS // nf
    rows = nf * ROWS
    half = rows // 2
    total = rows * LANES
    later, earlier = lax.rem(tm + 1, nt), lax.rem(tm + nt - 1, nt)

    def remote(src, dst, send, recv, **to):
        return pltpu.make_async_remote_copy(
            src_ref=src, dst_ref=dst, send_sem=send, recv_sem=recv, device_id=to, device_id_type=MESH
        )

    barrier = pltpu.get_barrier_semaphore()

    def greet_fiber(j, c):
        pl.semaphore_signal(
            barrier, inc=1, device_id={"fiber": lax.rem(me + j, nf)}, device_id_type=MESH
        )
        return c

    def greet_tm(j, c):
        pl.semaphore_signal(
            barrier, inc=1, device_id={"tm": lax.rem(tm + j, nt)}, device_id_type=MESH
        )
        return c

    lax.fori_loop(1, nt, greet_tm, 0)
    lax.fori_loop(1, nf, greet_fiber, 0)

    loads = [
        pltpu.make_async_copy(src, dst, load_sem.at[i])
        for i, (src, dst) in enumerate(
            [
                (ana_far, ana_raw),
                (strain_far, strain),
                (outer_far, outer_raw),
                (fwd_far, fwd_raw),
                (inv_far, inv_raw),
                (syn_far, syn_raw),
                (step_far, step),
                (turn_far, turn),
                (cut_far, cut),
                (sta_far, chan.at[0]),
                (lta_far, chan.at[1]),
                (drift_far, chan.at[2]),
                (limit_far, chan.at[3]),
            ]
        )
    ]
    for load in loads:
        load.start()

    def rates(i, at):
        return chan[i, at, :].astype(F32)

    pl.semaphore_wait(barrier, nf - 1 + nt - 1)

    chunks = 4
    wide = ROWS // chunks

    def rim_copy(c):
        span = pl.ds(c * wide * LANES, wide * LANES)
        return remote(strain_far.at[:, span], rim.at[:, span], rim_s.at[c], rim_r.at[c], tm=later)

    for chunk in range(chunks):
        rim_copy(chunk).start()

    for load in loads[:6]:
        load.wait()
    high, low = split(ana_raw[...])
    ana[...] = jnp.concatenate([high, low], axis=0)
    high, low = split(syn_raw[...])
    syn[...] = jnp.concatenate([high, high, low], axis=1)
    for raw, table in ((fwd_raw, fwd), (inv_raw, inv)):
        high, low = split(raw[...])
        table[...] = jnp.concatenate([high, high, low], axis=0)
    high, low = split(outer_raw[...])
    outer[...] = jnp.concatenate([high, high, low], axis=1)

    peak = jnp.zeros((1, 2 * LANES), F32)
    for chunk in range(chunks):
        rim_copy(chunk).wait_recv()
        for q in range(chunk * wide, (chunk + 1) * wide, 2):
            cols = slice(q * LANES, (q + 2) * LANES)
            before = jnp.where(tm > 0, rim[:, cols].astype(F32), 0.0).astype(BF16)
            frame = jnp.concatenate([before, strain[:, cols]], axis=0)
            both = jnp.dot(ana[...], frame, preferred_element_type=F32)
            got = both[:FRAME] + both[FRAME:]
            spec[:, q, :] = got[:, :LANES]
            spec[:, q + 1, :] = got[:, LANES:]
            peak = jnp.maximum(peak, jnp.max(jnp.abs(got), axis=0, keepdims=True))
    peak = peak_of(peak)
    gain = TOP / peak
    scs1[0] = jnp.broadcast_to(peak * (1.0 / TOP), (1, LANES))
    scr1[me] = scs1[0]

    def code1(i, c):
        at = pl.ds(i * 8, 8)
        snd1[at, :, 0:LANES] = coded(spec[at], gain)
        snd1[at, :, LANES : 2 * LANES] = coded(spec[pl.ds(BINS + i * 8, 8)], gain)
        return c

    def scale1(j):
        to = lax.rem(me + j, nf)
        return remote(scs1.at[0], scr1.at[me], c1s.at[j], c1r.at[j], fiber=to)

    def data1(b, j):
        to = lax.rem(me + j, nf)
        return remote(
            snd1.at[to * per + b],
            rcv1.at[b, pl.ds(pl.multiple_of(me * ROWS, ROWS), ROWS), :],
            s1s.at[b, j],
            s1r.at[b, j],
            fiber=to,
        )

    def from1(b, j):
        back = lax.rem(me + nf - j, nf)
        return remote(
            snd1.at[0],
            rcv1.at[b, pl.ds(pl.multiple_of(back * ROWS, ROWS), ROWS), :],
            s1s.at[b, j],
            s1r.at[b, j],
            fiber=back,
        )

    def out_scale(j, c):
        scale1(j).start()
        return c

    lax.fori_loop(1, nf, out_scale, 0)
    lax.fori_loop(0, BINS // 8, code1, 0)

    def out_bins(b, c):
        def out_peer(j, c):
            data1(b, j).start()
            return c

        lax.fori_loop(1, nf, out_peer, 0)
        rcv1[b, pl.ds(pl.multiple_of(me * ROWS, ROWS), ROWS), :] = snd1[me * per + b]
        return c

    lax.fori_loop(0, per, out_bins, 0)

    def in_scale(j, c):
        back = lax.rem(me + nf - j, nf)
        remote(scs1.at[0], scr1.at[back], c1s.at[j], c1r.at[j], fiber=back).wait_recv()
        return c

    lax.fori_loop(1, nf, in_scale, 0)

    for load in loads[6:]:
        load.wait()
    peers = nf // 2

    def scale2(b, blk, to):
        j = lax.rem(to - me + nf, nf)
        return remote(
            scs2.at[b, blk], scr2.at[me * per + b], c2s.at[b, j], c2r.at[b, j], fiber=to
        )

    def data2(b, to):
        j = lax.rem(to - me + nf, nf)
        return remote(
            snd2.at[b, pl.ds(pl.multiple_of(to * ROWS, ROWS), ROWS), :],
            rcv2.at[me * per + b],
            s2s.at[b, j],
            s2r.at[b, j],
            fiber=to,
        )

    lane = lax.broadcasted_iota(jnp.int32, (half, LANES), 1)
    row = lax.broadcasted_iota(jnp.int32, (half, LANES), 0)

    def parts(x):
        return x[:, :LANES], x[:, LANES:]

    def put(ref, e, at, size, x):
        high, low = split(x)
        for i, part in enumerate((high, low, high)):
            ref[e, pl.ds(pl.multiple_of(i * half + at, ROWS), size), :] = part

    def one_bin(b, c):
        def in_peer(j, c):
            from1(b, j).wait_recv()
            return c

        lax.fori_loop(1, nf, in_peer, 0)
        limit_k = cut[me * per + b]

        def values(p):
            x = rcv1[b, pl.ds(pl.multiple_of(p * ROWS, ROWS), ROWS), :].astype(F32)
            return x * jnp.concatenate([scr1[p], scr1[p]], axis=1)

        def decode(g, c):
            for i in range(GROUP):
                p = g * GROUP + i
                at = pl.multiple_of(p * ROWS, ROWS)
                early, late = values(p), values(p + peers)
                wr, wi = parts(step[pl.ds(at, ROWS), :])
                put(x3, 0, at, ROWS, early + late)
                re, im = parts(early - late)
                x = jnp.concatenate([re * wr - im * wi, re * wi + im * wr], axis=1)
                put(x3, 1, at, ROWS, x)
            return c

        lax.fori_loop(0, peers // GROUP, decode, 0)

        for e in range(2):
            pq = jnp.dot(outer[...], x3[e], preferred_element_type=F32)
            pr, pi = parts(pq[:half])
            qr, qi = parts(pq[half:])
            re, im = pr - qi, pi + qr
            tr, ti = parts(turn[e * half : (e + 1) * half, :])
            y = jnp.concatenate([re * tr - im * ti, re * ti + im * tr], axis=1)
            wr, wi = parts(jnp.dot(across(y), fwd[...], preferred_element_type=F32))
            k = 2 * row + e + rows * lane
            keep = jnp.minimum(k, total - k) <= limit_k
            w = jnp.concatenate([jnp.where(keep, wr, 0.0), jnp.where(keep, wi, 0.0)], axis=1)
            re, im = parts(jnp.dot(across(w), inv[...], preferred_element_type=F32))
            put(z3, e, 0, half, jnp.concatenate([re * tr + im * ti, im * tr - re * ti], axis=1))

        back = []
        for e in range(2):
            pq = jnp.dot(outer[...], z3[e], preferred_element_type=F32)
            pr, pi = parts(pq[:half])
            qr, qi = parts(pq[half:])
            back.append((pr + qi, pi - qr))
        (ur, ui), (re, im) = back
        wr, wi = parts(step[...])
        vr, vi = re * wr + im * wi, im * wr - re * wi
        for blk, x in enumerate(
            (jnp.concatenate([ur + vr, ui + vi], axis=1), jnp.concatenate([ur - vr, ui - vi], axis=1))
        ):
            top = peak_of(x)
            scs2[b, blk] = jnp.broadcast_to(top * (1.0 / TOP), (1, LANES))
            snd2[b, blk * half : (blk + 1) * half, :] = coded(x, TOP / top)

        def out_peer(j, c):
            to = lax.rem(me + j, nf)
            scale2(b, to // peers, to).start()
            data2(b, to).start()
            return c

        lax.fori_loop(1, nf, out_peer, 0)
        scr2[me * per + b] = scs2[b, me // peers]
        rcv2[me * per + b] = snd2[b, pl.ds(pl.multiple_of(me * ROWS, ROWS), ROWS), :]
        return c

    lax.fori_loop(0, per, one_bin, 0)

    def in_back(j, c):
        back = lax.rem(me + nf - j, nf)

        def in_bin(b, c):
            f = back * per + b
            remote(scs2.at[0, 0], scr2.at[f], c2s.at[b, j], c2r.at[b, j], fiber=back).wait_recv()
            remote(
                snd2.at[0, pl.ds(0, ROWS), :], rcv2.at[f], s2s.at[b, j], s2r.at[b, j], fiber=back
            ).wait_recv()
            return c

        lax.fori_loop(0, per, in_bin, 0)
        return c

    lax.fori_loop(1, nf, in_back, 0)

    def decode2(i, c):
        at = pl.ds(i * 8, 8)
        x = rcv2[at].astype(F32)
        deco[0, at] = x[:, :, :LANES] * scr2[at]
        deco[1, at] = x[:, :, LANES:] * scr2[at]
        return c

    lax.fori_loop(0, BINS // 8, decode2, 0)

    def spill(c):
        span = pl.ds(c * wide, wide)
        return remote(sps.at[span], spr.at[span], sp_s.at[c], sp_r.at[c], tm=earlier)

    def spill_scale(c):
        return remote(sss.at[c], ssr.at[c], ss_s.at[c], ss_r.at[c], tm=earlier)

    for chunk in range(chunks):
        top = jnp.full((1, 1), 1e-30, F32)
        for q in range(chunk * wide, (chunk + 1) * wide, 2):
            x = jnp.concatenate(
                [
                    jnp.concatenate([deco[0, :, q, :], deco[1, :, q, :]], axis=0),
                    jnp.concatenate([deco[0, :, q + 1, :], deco[1, :, q + 1, :]], axis=0),
                ],
                axis=1,
            )
            high, low = split(x)
            got = jnp.dot(
                syn[...], jnp.concatenate([high, low, high], axis=0), preferred_element_type=F32
            )
            for i in range(2):
                head[q + i] = got[:HOP, i * LANES : (i + 1) * LANES]
                tail[q + i] = got[HOP:, i * LANES : (i + 1) * LANES]
            top = jnp.maximum(top, peak_of(got[:HOP]))
        sss[chunk] = jnp.broadcast_to(top * (1.0 / TOP), (1, LANES))
        spill_scale(chunk).start()
        for q in range(chunk * wide, (chunk + 1) * wide):
            sps[q] = coded(head[q], TOP / top)
        spill(chunk).start()

    has_next = jnp.where(tm < nt - 1, 1.0, 0.0).astype(F32)
    seg_id = lax.broadcasted_iota(jnp.int32, (8, LANES), 0)

    def shifted(x, by, fill):
        return jnp.where(seg_id >= by, pltpu.roll(x, by, 0), fill)

    def rate_of(length):
        return 1.0 - 1.0 / length

    def natural(g, vectors):
        for i in range(8):
            temp[g, pl.ds(i, 8, stride=8), :] = vectors[i]
        return temp[g]

    def grouped(one):
        def group(i, c):
            for g in range(GROUP):
                one(i * GROUP + g, g)
            return c

        return group

    for chunk in range(chunks):
        spill_scale(chunk).wait_recv()
        spill(chunk).wait_recv()

        def scan_row(q, g):
            at = pl.ds(q, 1)
            cols = pl.ds(pl.multiple_of(q * LANES, LANES), LANES)
            heads = spr[q].astype(F32) * (ssr[chunk] * has_next)
            rounded = (tail[q] + heads).astype(BF16).astype(F32)
            part = [rounded[8 * i : 8 * i + 8] for i in range(8)]
            filtered[:, cols] = natural(g, part).astype(BF16)
            energy = [v * v for v in part]
            for s in range(2):
                keep = jnp.broadcast_to(rate_of(rates(s, at)), (8, LANES))
                gain = 1.0 - keep
                level = gain * energy[0]
                lev[s, q, 0:8] = level
                for i in range(1, 8):
                    level = keep * level + gain * energy[i]
                    lev[s, q, 8 * i : 8 * i + 8] = level
                power = keep * keep
                power = power * power
                power = power * power
                for by in (1, 2, 4):
                    level = level + power * shifted(level, by, 0.0)
                    power = power * power
                seg[s, q] = shifted(level, 1, 0.0)
                cars[s, at, :] = level[7:8]

        for g in range(wide):
            scan_row(chunk * wide + g, g)

    stores = [
        pltpu.make_async_copy(src, dst, store_sem.at[i])
        for i, (src, dst) in enumerate([(filtered, filtered_far), (ratio, ratio_far), (ph, ph_far)])
    ]
    stores[0].start()

    def to_later(snd, rcv, send, recv, j):
        return remote(snd, rcv.at[tm], send.at[j], recv.at[j], tm=lax.rem(tm + j, nt))

    def from_earlier(snd, rcv, send, recv, j):
        back = lax.rem(tm + nt - j, nt)
        return remote(snd, rcv.at[back], send.at[j], recv.at[j], tm=back)

    def pass_on(snd, rcv, send, recv):
        def out(j, c):
            to_later(snd, rcv, send, recv, j).start()
            return c

        lax.fori_loop(1, nt - tm, out, 0)

        def come(j, c):
            from_earlier(snd, rcv, send, recv, j).wait_recv()
            return c

        lax.fori_loop(1, tm + 1, come, 0)

    pass_on(cars, carr, ca_s, ca_r)
    decay = []
    for s in range(2):
        power = rate_of(chan[s].astype(F32))
        for _ in range(6):
            power = power * power
        decay.append(power)

    def lap(k, state):
        return tuple(decay[s] * state[s] + carr[k, s] for s in range(2))

    ones = jnp.ones((ROWS, LANES), F32)
    start = lax.fori_loop(0, tm, lap, (ones, ones))
    head[0, 0:ROWS] = start[0]
    head[1, 0:ROWS] = start[1]

    def climb_row(q, g):
        at = pl.ds(q, 1)
        cols = pl.ds(pl.multiple_of(q * LANES, LANES), LANES)
        avg = []
        for s in range(2):
            keep = jnp.broadcast_to(rate_of(rates(s, at)), (8, LANES))
            carry = jnp.broadcast_to(head[s, at, :], (8, LANES))
            power = keep * keep
            power = power * power
            power = power * power
            for bit in (1, 2, 4):
                carry = jnp.where((seg_id // bit) % 2 == 1, carry * power, carry)
                power = power * power
            entry = seg[s, q] + carry
            values = []
            for i in range(8):
                entry = entry * keep
                values.append(lev[s, q, 8 * i : 8 * i + 8] + entry)
            avg.append(values)
        quotient = [avg[0][i] / avg[1][i] for i in range(8)]
        ratio[:, cols] = natural(g, quotient)
        rate = jnp.broadcast_to(0.5 + rates(2, at) * (1.0 / 64.0), (8, LANES))
        climb = quotient[0] - rate
        low = climb
        climbs, lows = [climb], [low]
        for i in range(1, 8):
            climb = climb + (quotient[i] - rate)
            low = jnp.minimum(low, climb)
            climbs.append(climb)
            lows.append(low)
        whole = climb
        for by in (1, 2, 4):
            whole = whole + shifted(whole, by, 0.0)
        base = shifted(whole, 1, 0.0)
        least = base + low
        for by in (1, 2, 4):
            least = jnp.minimum(least, shifted(least, by, jnp.inf))
        floor = shifted(least, 1, jnp.inf)
        for i in range(8):
            up = base + climbs[i]
            lev[0, q, 8 * i : 8 * i + 8] = up
            lev[1, q, 8 * i : 8 * i + 8] = jnp.minimum(floor, base + lows[i])
        sums[0, at, :] = whole[7:8]
        sums[1, at, :] = least[7:8]

    lax.fori_loop(0, ROWS // GROUP, grouped(climb_row), 0)

    stores[1].start()
    pass_on(sums, sumr, su_s, su_r)

    def lap2(k, state):
        total_up, low = state
        return total_up + sumr[k, 0], jnp.minimum(low, total_up + sumr[k, 1])

    zeros = jnp.zeros((ROWS, LANES), F32)
    before, low = lax.fori_loop(0, tm, lap2, (zeros, zeros))
    head[2, 0:ROWS] = before
    head[3, 0:ROWS] = low

    def ph_row(q, g):
        at = pl.ds(q, 1)
        cols = pl.ds(pl.multiple_of(q * LANES, LANES), LANES)
        base = jnp.broadcast_to(head[2, at, :], (8, LANES))
        low = jnp.broadcast_to(head[3, at, :], (8, LANES))
        scale = jnp.broadcast_to(1.0 / rates(3, at), (8, LANES))
        out = []
        for i in range(8):
            climb = base + lev[0, q, 8 * i : 8 * i + 8]
            lowest = jnp.minimum(low, base + lev[1, q, 8 * i : 8 * i + 8])
            out.append((climb - lowest) * scale)
        ph[:, cols] = natural(g, out)

    lax.fori_loop(0, ROWS // GROUP, grouped(ph_row), 0)

    stores[2].start()

    for chunk in range(chunks):
        rim_copy(chunk).wait_send()

    def sent1(j, c):
        scale1(j).wait_send()

        def sent_bin(b, c):
            data1(b, j).wait_send()
            to = lax.rem(me + j, nf)
            scale2(b, 0, to).wait_send()
            data2(b, to).wait_send()
            return c

        lax.fori_loop(0, per, sent_bin, 0)
        return c

    lax.fori_loop(1, nf, sent1, 0)
    for chunk in range(chunks):
        spill_scale(chunk).wait_send()
        spill(chunk).wait_send()

    def sent_on(j, c):
        to_later(sums, carr, ca_s, ca_r, j).wait_send()
        to_later(sums, sumr, su_s, su_r, j).wait_send()
        return c

    lax.fori_loop(1, nt - tm, sent_on, 0)
    for store in stores:
        store.wait()


def hand_over(*refs):
    copies = [pltpu.make_async_copy(refs[i], refs[3 + i], refs[6].at[i]) for i in range(3)]
    for copy in copies:
        copy.start()
    for copy in copies:
        copy.wait()


def body(nf, nt, strain, fan_cut, sta_len, lta_len, drift_code, threshold):
    per = BINS // nf
    rows = nf * ROWS
    total = rows * LANES
    half = rows // 2
    tabs = [jnp.asarray(t) for t in tables(total)]
    per_chan = [v.reshape(ROWS, LANES) for v in (sta_len, lta_len, drift_code, threshold)]
    far = pl.BlockSpec(memory_space=pl.ANY)
    dma = pltpu.SemaphoreType.DMA
    i16 = jnp.int16
    chans = ROWS * LANES
    results = pl.pallas_call(
        functools.partial(kernel, nf, nt),
        out_shape=(
            jax.ShapeDtypeStruct((HOP, chans), BF16),
            jax.ShapeDtypeStruct((HOP, chans), F32),
            jax.ShapeDtypeStruct((HOP, chans), F32),
        ),
        in_specs=[far] * 13,
        out_specs=(far, far, far),
        scratch_shapes=[
            pltpu.VMEM((HOP, chans), BF16),
            pltpu.SMEM((BINS,), jnp.int32),
            pltpu.VMEM((4, ROWS, LANES), jnp.int32),
        ]
        + [pltpu.VMEM(t.shape, F32) for t in tabs]
        + [
            pltpu.VMEM((2 * FRAME, FRAME), BF16),
            pltpu.VMEM((rows, 3 * half), BF16),
            pltpu.VMEM((6 * LANES, 2 * LANES), BF16),
            pltpu.VMEM((6 * LANES, 2 * LANES), BF16),
            pltpu.VMEM((FRAME, 3 * FRAME), BF16),
            pltpu.VMEM((HOP, chans), BF16),
            pltpu.VMEM((HOP, chans), F32),
            pltpu.VMEM((HOP, chans), F32),
            pltpu.VMEM((HOP, chans), BF16),
            pltpu.VMEM((FRAME, ROWS, LANES), F32),
            pltpu.VMEM((BINS, ROWS, 2 * LANES), i16),
            pltpu.VMEM((per, rows, 2 * LANES), i16),
            pltpu.VMEM((1, 1, LANES), F32),
            pltpu.VMEM((nf, 1, LANES), F32),
            pltpu.VMEM((2, 3 * half, 2 * LANES), BF16),
            pltpu.VMEM((2, 3 * half, 2 * LANES), BF16),
            pltpu.VMEM((per, rows, 2 * LANES), i16),
            pltpu.VMEM((BINS, ROWS, 2 * LANES), i16),
            pltpu.VMEM((per, 2, 1, LANES), F32),
            pltpu.VMEM((BINS, 1, LANES), F32),
            pltpu.VMEM((2, BINS, ROWS, LANES), F32),
            pltpu.VMEM((ROWS, HOP, LANES), F32),
            pltpu.VMEM((ROWS, HOP, LANES), F32),
            pltpu.VMEM((ROWS, HOP, LANES), i16),
            pltpu.VMEM((ROWS, HOP, LANES), i16),
            pltpu.VMEM((4, 1, LANES), F32),
            pltpu.VMEM((4, 1, LANES), F32),
            pltpu.VMEM((2, ROWS, HOP, LANES), F32),
            pltpu.VMEM((2, ROWS, 8, LANES), F32),
            pltpu.VMEM((2, ROWS, LANES), F32),
            pltpu.VMEM((nt, 2, ROWS, LANES), F32),
            pltpu.VMEM((2, ROWS, LANES), F32),
            pltpu.VMEM((nt, 2, ROWS, LANES), F32),
            pltpu.VMEM((GROUP, HOP, LANES), F32),
            dma((4,)),
            dma((4,)),
            dma((per, nf)),
            dma((per, nf)),
            dma((nf,)),
            dma((nf,)),
            dma((per, nf)),
            dma((per, nf)),
            dma((per, nf)),
            dma((per, nf)),
            dma((4,)),
            dma((4,)),
            dma((4,)),
            dma((4,)),
            dma((nt,)),
            dma((nt,)),
            dma((nt,)),
            dma((nt,)),
            dma((13,)),
            dma((3,)),
        ],
        compiler_params=pltpu.CompilerParams(
            collective_id=0, has_side_effects=True, vmem_limit_bytes=64 * 1024 * 1024
        ),
    )(strain, fan_cut, *per_chan, *tabs)
    return pl.pallas_call(
        hand_over,
        out_shape=tuple(jax.ShapeDtypeStruct(r.shape, r.dtype) for r in results),
        in_specs=[far] * 3,
        out_specs=(far,) * 3,
        scratch_shapes=[dma((3,))],
        compiler_params=pltpu.CompilerParams(vmem_limit_bytes=64 * 1024 * 1024),
    )(*results)


def solution(mesh):
    return jax.shard_map(
        functools.partial(body, mesh.shape["fiber"], mesh.shape["tm"]),
        mesh=mesh,
        in_specs=(P("tm", "fiber"), P(), P("fiber"), P("fiber"), P("fiber"), P("fiber")),
        out_specs=(P("tm", "fiber"), P("tm", "fiber"), P("tm", "fiber")),
        check_vma=False,
    )
```

time: 84.7 us -> 109 us (1.29); the launches traced: 83.1 us -> 109 us
  Pallas kernels: 72.4 us -> 108 us
  local copies, waits for them, and re-layouts: 8.66 us -> 0 us
  other arithmetic: 1.43 us -> 0 us
    pallas_call x0 -> x1, Pallas kernels: none -> 40.8 us  [body(): pl.pallas_call(hand_over, out_shape=tuple((jax.ShapeDtypeStruct(r.shape,...]
    unnamed x17 -> x0, local copies, waits for them, and re-layouts: 8.66 us -> none
    pallas_call x1, Pallas kernels: 72.4 us -> 67.5 us  [body(): pl.pallas_call(functools.partial(kernel, nf, nt), out_shape=(jax.ShapeDty...]
    reshape x2 -> x0, other arithmetic: 1.43 us -> none  [body(): v.astype(F32).reshape(ROWS, LANES)]
where the time goes in v2:
time: 109 us
  Pallas kernels  108 us (99%)
    pallas_call x1, Pallas kernels, body(): pl.pallas_call(functools.partial(kernel, nf, nt), out_shape=(jax.ShapeDty...  67.5 us
    pallas_call x1, Pallas kernels, body(): pl.pallas_call(hand_over, out_shape=tuple((jax.ShapeDtypeStruct(r.shape,...  40.8 us

profile of v2, /device:TPU:1, one launch (start us, length us, event | category | flops | bytes accessed | tf_op | source)
XLA Modules:
  0.0 109.0 jit_solution(9155841487484287849)
XLA Ops:
  0.6 67.5 %shard_map.148 = (bf16[64,2048]{1,0:T(8,128)(2,1)}, f32[64,2048]{1,0:T(8,128)}, f32[64,2048]{1,0:T(8,128)}) custom-call(bf16[64,2048]{1,0:T(8,128)(2,1)} %refs_0_.1, s32[64]{0:T(128)} %refs_1_.1, s32[16,128]{1,0:T(8,128)} %bitcast.4, s32[16,128]{1,0:T(8,128)} %bitcast.5, s32[16,128]{1,0:T(8,128)} %bitcast.6, s32[16,128]{1,0:T(8,128)} %bitcast.7, ...), custom_call_target="tpu_custom_call" | custom-call | tf_op jit(solution)/shard_map/pallas_call | solution.py:693
  68.2 40.8 %shard_map.149 = (bf16[64,2048]{1,0:T(8,128)(2,1)}, f32[64,2048]{1,0:T(8,128)}, f32[64,2048]{1,0:T(8,128)}) custom-call(bf16[64,2048]{1,0:T(8,128)(2,1)} %get-tuple-element.6.refs_0_, f32[64,2048]{1,0:T(8,128)} %get-tuple-element.7.refs_1_, f32[64,2048]{1,0:T(8,128)} %get-tuple-element.8.refs_2_), custom_call_target="tpu_custom_call" | custom-call | tf_op jit(solution)/shard_map/pallas_call | solution.py:768

commit v3 on v2

--- a/solution.py
+++ b/solution.py
@@ -69,6 +69,12 @@
     return jnp.maximum(top, 1e-30)
 
 
+def in_order(temp, g, vectors):
+    for i in range(8):
+        temp[g, pl.ds(i, 8, stride=8), :] = vectors[i]
+    return temp[g]
+
+
 def coded(x, gain):
     return jnp.round(x * gain).astype(jnp.int32).astype(jnp.int16)
 
@@ -84,7 +90,6 @@
         sta_far,
         lta_far,
         drift_far,
-        limit_far,
         ana_far,
         outer_far,
         fwd_far,
@@ -94,7 +99,8 @@
         turn_far,
         filtered_far,
         ratio_far,
-        ph_far,
+        lev_far,
+        prior_far,
         strain,
         cut,
         chan,
@@ -112,7 +118,6 @@
         syn,
         filtered,
         ratio,
-        ph,
         rim,
         spec,
         snd1,
@@ -206,7 +211,6 @@
                 (sta_far, chan.at[0]),
                 (lta_far, chan.at[1]),
                 (drift_far, chan.at[2]),
-                (limit_far, chan.at[3]),
             ]
         )
     ]
@@ -240,97 +244,115 @@
     high, low = split(outer_raw[...])
     outer[...] = jnp.concatenate([high, high, low], axis=1)
 
-    peak = jnp.zeros((1, 2 * LANES), F32)
-    for chunk in range(chunks):
-        rim_copy(chunk).wait_recv()
-        for q in range(chunk * wide, (chunk + 1) * wide, 2):
-            cols = slice(q * LANES, (q + 2) * LANES)
-            before = jnp.where(tm > 0, rim[:, cols].astype(F32), 0.0).astype(BF16)
-            frame = jnp.concatenate([before, strain[:, cols]], axis=0)
-            both = jnp.dot(ana[...], frame, preferred_element_type=F32)
-            got = both[:FRAME] + both[FRAME:]
-            spec[:, q, :] = got[:, :LANES]
-            spec[:, q + 1, :] = got[:, LANES:]
-            peak = jnp.maximum(peak, jnp.max(jnp.abs(got), axis=0, keepdims=True))
-    peak = peak_of(peak)
-    gain = TOP / peak
-    scs1[0] = jnp.broadcast_to(peak * (1.0 / TOP), (1, LANES))
-    scr1[me] = scs1[0]
-
-    def code1(i, c):
-        at = pl.ds(i * 8, 8)
-        snd1[at, :, 0:LANES] = coded(spec[at], gain)
-        snd1[at, :, LANES : 2 * LANES] = coded(spec[pl.ds(BINS + i * 8, 8)], gain)
-        return c
-
-    def scale1(j):
+    tall = ROWS // 2
+
+    def scale1(h, j):
         to = lax.rem(me + j, nf)
-        return remote(scs1.at[0], scr1.at[me], c1s.at[j], c1r.at[j], fiber=to)
-
-    def data1(b, j):
+        return remote(scs1.at[h], scr1.at[h, me], c1s.at[h, j], c1r.at[h, j], fiber=to)
+
+    def data1(i, j):
         to = lax.rem(me + j, nf)
-        return remote(
-            snd1.at[to * per + b],
-            rcv1.at[b, pl.ds(pl.multiple_of(me * ROWS, ROWS), ROWS), :],
-            s1s.at[b, j],
-            s1r.at[b, j],
-            fiber=to,
-        )
-
-    def from1(b, j):
+        if i == 0:
+            src, dst = snd1.at[0, pl.ds(to * per, per)], rcv1.at[0, me]
+        else:
+            src, dst = snd1.at[1, to * per + i - 1], rcv1.at[1, me, i - 1]
+        return remote(src, dst, s1s.at[i, j], s1r.at[i, j], fiber=to)
+
+    def from1(i, j):
         back = lax.rem(me + nf - j, nf)
-        return remote(
-            snd1.at[0],
-            rcv1.at[b, pl.ds(pl.multiple_of(back * ROWS, ROWS), ROWS), :],
-            s1s.at[b, j],
-            s1r.at[b, j],
-            fiber=back,
-        )
-
-    def out_scale(j, c):
-        scale1(j).start()
-        return c
-
-    lax.fori_loop(1, nf, out_scale, 0)
-    lax.fori_loop(0, BINS // 8, code1, 0)
-
-    def out_bins(b, c):
-        def out_peer(j, c):
-            data1(b, j).start()
+        if i == 0:
+            src, dst = snd1.at[0, pl.ds(0, per)], rcv1.at[0, back]
+        else:
+            src, dst = snd1.at[1, 0], rcv1.at[1, back, i - 1]
+        return remote(src, dst, s1s.at[i, j], s1r.at[i, j], fiber=back)
+
+    def each_peer(act):
+        def one(j, c):
+            act(j)
             return c
 
-        lax.fori_loop(1, nf, out_peer, 0)
-        rcv1[b, pl.ds(pl.multiple_of(me * ROWS, ROWS), ROWS), :] = snd1[me * per + b]
-        return c
-
-    lax.fori_loop(0, per, out_bins, 0)
-
-    def in_scale(j, c):
+        lax.fori_loop(1, nf, one, 0)
+
+    for h in range(2):
+        peak = jnp.zeros((1, 2 * LANES), F32)
+        for chunk in range(h * chunks // 2, (h + 1) * chunks // 2):
+            rim_copy(chunk).wait_recv()
+            for q in range(chunk * wide, (chunk + 1) * wide, 2):
+                cols = slice(q * LANES, (q + 2) * LANES)
+                before = jnp.where(tm > 0, rim[:, cols].astype(F32), 0.0).astype(BF16)
+                frame = jnp.concatenate([before, strain[:, cols]], axis=0)
+                both = jnp.dot(ana[...], frame, preferred_element_type=F32)
+                got = both[:FRAME] + both[FRAME:]
+                spec[:, q, :] = got[:, :LANES]
+                spec[:, q + 1, :] = got[:, LANES:]
+                peak = jnp.maximum(peak, jnp.max(jnp.abs(got), axis=0, keepdims=True))
+        peak = peak_of(peak)
+        gain = TOP / peak
+        scs1[h] = jnp.broadcast_to(peak * (1.0 / TOP), (1, LANES))
+        scr1[h, me] = scs1[h]
+
+        def code1(i, c):
+            half_rows = slice(h * tall, (h + 1) * tall)
+            re = spec[pl.ds(i * 8, 8), half_rows, :]
+            im = spec[pl.ds(BINS + i * 8, 8), half_rows, :]
+            snd1[h, pl.ds(i * 8, 8)] = coded(jnp.concatenate([re, im], axis=1), gain)
+            return c
+
+        lax.fori_loop(0, BINS // 8, code1, 0)
+        if h == 0:
+
+            def send0(j):
+                scale1(0, j).start()
+                data1(0, j).start()
+
+            each_peer(send0)
+        else:
+
+            def send1(j):
+                scale1(1, j).start()
+                data1(1, j).start()
+
+            each_peer(send1)
+            for b in range(1, per):
+                each_peer(lambda j: data1(1 + b, j).start())
+        rcv1[h, me] = snd1[h, pl.ds(me * per, per)]
+
+    def first_scales(j):
         back = lax.rem(me + nf - j, nf)
-        remote(scs1.at[0], scr1.at[back], c1s.at[j], c1r.at[j], fiber=back).wait_recv()
-        return c
-
-    lax.fori_loop(1, nf, in_scale, 0)
+        for h in range(2):
+            remote(
+                scs1.at[h], scr1.at[h, back], c1s.at[h, j], c1r.at[h, j], fiber=back
+            ).wait_recv()
+
+    each_peer(lambda j: from1(0, j).wait_recv())
 
     for load in loads[6:]:
         load.wait()
     peers = nf // 2
 
-    def scale2(b, blk, to):
-        j = lax.rem(to - me + nf, nf)
+    final = per - 1
+
+    def scale2(b, j):
+        to = lax.rem(me + j, nf)
         return remote(
-            scs2.at[b, blk], scr2.at[me * per + b], c2s.at[b, j], c2r.at[b, j], fiber=to
+            scs2.at[b, to // peers], scr2.at[me * per + b], c2s.at[b, j], c2r.at[b, j], fiber=to
         )
 
-    def data2(b, to):
-        j = lax.rem(to - me + nf, nf)
-        return remote(
-            snd2.at[b, pl.ds(pl.multiple_of(to * ROWS, ROWS), ROWS), :],
-            rcv2.at[me * per + b],
-            s2s.at[b, j],
-            s2r.at[b, j],
-            fiber=to,
-        )
+    def data2(i, j):
+        to = lax.rem(me + j, nf)
+        if i < final:
+            src, dst = snd2.at[i, to], rcv2.at[me * per + i]
+        else:
+            src, dst = snd2.at[final, to, i - final], rcv2.at[me * per + final, i - final]
+        return remote(src, dst, s2s.at[i, j], s2r.at[i, j], fiber=to)
+
+    def from2(i, j):
+        back = lax.rem(me + nf - j, nf)
+        if i < final:
+            src, dst = snd2.at[i, 0], rcv2.at[back * per + i]
+        else:
+            src, dst = snd2.at[final, 0, 0], rcv2.at[back * per + final, i - final]
+        return remote(src, dst, s2s.at[i, j], s2r.at[i, j], fiber=back)
 
     lane = lax.broadcasted_iota(jnp.int32, (half, LANES), 1)
     row = lax.broadcasted_iota(jnp.int32, (half, LANES), 0)
@@ -343,17 +365,18 @@
         for i, part in enumerate((high, low, high)):
             ref[e, pl.ds(pl.multiple_of(i * half + at, ROWS), size), :] = part
 
-    def one_bin(b, c):
-        def in_peer(j, c):
-            from1(b, j).wait_recv()
-            return c
-
-        lax.fori_loop(1, nf, in_peer, 0)
+    for b in range(per):
+        if b == 0:
+            each_peer(first_scales)
+        each_peer(lambda j: from1(1 + b, j).wait_recv())
         limit_k = cut[me * per + b]
 
         def values(p):
-            x = rcv1[b, pl.ds(pl.multiple_of(p * ROWS, ROWS), ROWS), :].astype(F32)
-            return x * jnp.concatenate([scr1[p], scr1[p]], axis=1)
+            pieces = [rcv1[h, p, b].astype(F32) * scr1[h, p] for h in range(2)]
+            return jnp.concatenate(
+                [jnp.concatenate([x[i * tall : (i + 1) * tall] for x in pieces], 0) for i in range(2)],
+                axis=1,
+            )
 
         def decode(g, c):
             for i in range(GROUP):
@@ -392,50 +415,47 @@
         (ur, ui), (re, im) = back
         wr, wi = parts(step[...])
         vr, vi = re * wr + im * wi, im * wr - re * wi
-        for blk, x in enumerate(
-            (jnp.concatenate([ur + vr, ui + vi], axis=1), jnp.concatenate([ur - vr, ui - vi], axis=1))
-        ):
-            top = peak_of(x)
+        for blk, (re, im) in enumerate(((ur + vr, ui + vi), (ur - vr, ui - vi))):
+            top = peak_of(jnp.maximum(jnp.abs(re), jnp.abs(im)))
             scs2[b, blk] = jnp.broadcast_to(top * (1.0 / TOP), (1, LANES))
-            snd2[b, blk * half : (blk + 1) * half, :] = coded(x, TOP / top)
-
-        def out_peer(j, c):
-            to = lax.rem(me + j, nf)
-            scale2(b, to // peers, to).start()
-            data2(b, to).start()
+            re = re.reshape(peers, 2, tall, LANES)
+            im = im.reshape(peers, 2, tall, LANES)
+            code = coded(jnp.concatenate([re, im], axis=2), TOP / top)
+            snd2[b, blk * peers : (blk + 1) * peers] = code
+
+        def send2(j):
+            scale2(b, j).start()
+            data2(b, j).start()
+
+        each_peer(send2)
+        if b == final:
+            each_peer(lambda j: data2(per, j).start())
+        scr2[me * per + b] = scs2[b, me // peers]
+        rcv2[me * per + b] = snd2[b, me]
+
+    def second_scales(j):
+        back = lax.rem(me + nf - j, nf)
+        for b in range(per):
+            remote(
+                scs2.at[0, 0], scr2.at[back * per + b], c2s.at[b, j], c2r.at[b, j], fiber=back
+            ).wait_recv()
+
+    def back_again(h):
+        if h == 0:
+            for i in range(per):
+                each_peer(lambda j: from2(i, j).wait_recv())
+            each_peer(second_scales)
+        else:
+            each_peer(lambda j: from2(per, j).wait_recv())
+
+        def decode2(i, c):
+            at = pl.ds(i * 8, 8)
+            x = rcv2[at, h].astype(F32) * scr2[at]
+            deco[0, at, h * tall : (h + 1) * tall] = x[:, :tall]
+            deco[1, at, h * tall : (h + 1) * tall] = x[:, tall:]
             return c
 
-        lax.fori_loop(1, nf, out_peer, 0)
-        scr2[me * per + b] = scs2[b, me // peers]
-        rcv2[me * per + b] = snd2[b, pl.ds(pl.multiple_of(me * ROWS, ROWS), ROWS), :]
-        return c
-
-    lax.fori_loop(0, per, one_bin, 0)
-
-    def in_back(j, c):
-        back = lax.rem(me + nf - j, nf)
-
-        def in_bin(b, c):
-            f = back * per + b
-            remote(scs2.at[0, 0], scr2.at[f], c2s.at[b, j], c2r.at[b, j], fiber=back).wait_recv()
-            remote(
-                snd2.at[0, pl.ds(0, ROWS), :], rcv2.at[f], s2s.at[b, j], s2r.at[b, j], fiber=back
-            ).wait_recv()
-            return c
-
-        lax.fori_loop(0, per, in_bin, 0)
-        return c
-
-    lax.fori_loop(1, nf, in_back, 0)
-
-    def decode2(i, c):
-        at = pl.ds(i * 8, 8)
-        x = rcv2[at].astype(F32)
-        deco[0, at] = x[:, :, :LANES] * scr2[at]
-        deco[1, at] = x[:, :, LANES:] * scr2[at]
-        return c
-
-    lax.fori_loop(0, BINS // 8, decode2, 0)
+        lax.fori_loop(0, BINS // 8, decode2, 0)
 
     def spill(c):
         span = pl.ds(c * wide, wide)
@@ -445,6 +465,8 @@
         return remote(sss.at[c], ssr.at[c], ss_s.at[c], ss_r.at[c], tm=earlier)
 
     for chunk in range(chunks):
+        if chunk % (chunks // 2) == 0:
+            back_again(chunk // (chunks // 2))
         top = jnp.full((1, 1), 1e-30, F32)
         for q in range(chunk * wide, (chunk + 1) * wide, 2):
             x = jnp.concatenate(
@@ -478,9 +500,7 @@
         return 1.0 - 1.0 / length
 
     def natural(g, vectors):
-        for i in range(8):
-            temp[g, pl.ds(i, 8, stride=8), :] = vectors[i]
-        return temp[g]
+        return in_order(temp, g, vectors)
 
     def grouped(one):
         def group(i, c):
@@ -524,7 +544,7 @@
 
     stores = [
         pltpu.make_async_copy(src, dst, store_sem.at[i])
-        for i, (src, dst) in enumerate([(filtered, filtered_far), (ratio, ratio_far), (ph, ph_far)])
+        for i, (src, dst) in enumerate([(filtered, filtered_far), (ratio, ratio_far), (lev, lev_far)])
     ]
     stores[0].start()
 
@@ -612,6 +632,7 @@
     lax.fori_loop(0, ROWS // GROUP, grouped(climb_row), 0)
 
     stores[1].start()
+    stores[2].start()
     pass_on(sums, sumr, su_s, su_r)
 
     def lap2(k, state):
@@ -622,41 +643,22 @@
     before, low = lax.fori_loop(0, tm, lap2, (zeros, zeros))
     head[2, 0:ROWS] = before
     head[3, 0:ROWS] = low
-
-    def ph_row(q, g):
-        at = pl.ds(q, 1)
-        cols = pl.ds(pl.multiple_of(q * LANES, LANES), LANES)
-        base = jnp.broadcast_to(head[2, at, :], (8, LANES))
-        low = jnp.broadcast_to(head[3, at, :], (8, LANES))
-        scale = jnp.broadcast_to(1.0 / rates(3, at), (8, LANES))
-        out = []
-        for i in range(8):
-            climb = base + lev[0, q, 8 * i : 8 * i + 8]
-            lowest = jnp.minimum(low, base + lev[1, q, 8 * i : 8 * i + 8])
-            out.append((climb - lowest) * scale)
-        ph[:, cols] = natural(g, out)
-
-    lax.fori_loop(0, ROWS // GROUP, grouped(ph_row), 0)
-
-    stores[2].start()
+    last = pltpu.make_async_copy(head.at[pl.ds(2, 2), pl.ds(0, ROWS), :], prior_far, store_sem.at[3])
+    last.start()
 
     for chunk in range(chunks):
         rim_copy(chunk).wait_send()
 
-    def sent1(j, c):
-        scale1(j).wait_send()
-
-        def sent_bin(b, c):
-            data1(b, j).wait_send()
-            to = lax.rem(me + j, nf)
-            scale2(b, 0, to).wait_send()
-            data2(b, to).wait_send()
-            return c
-
-        lax.fori_loop(0, per, sent_bin, 0)
-        return c
-
-    lax.fori_loop(1, nf, sent1, 0)
+    def all_sent(j):
+        for h in range(2):
+            scale1(h, j).wait_send()
+        for b in range(per):
+            scale2(b, j).wait_send()
+        for i in range(per + 1):
+            data1(i, j).wait_send()
+            data2(i, j).wait_send()
+
+    each_peer(all_sent)
     for chunk in range(chunks):
         spill_scale(chunk).wait_send()
         spill(chunk).wait_send()
@@ -669,14 +671,67 @@
     lax.fori_loop(1, nt - tm, sent_on, 0)
     for store in stores:
         store.wait()
-
-
-def hand_over(*refs):
-    copies = [pltpu.make_async_copy(refs[i], refs[3 + i], refs[6].at[i]) for i in range(3)]
-    for copy in copies:
-        copy.start()
-    for copy in copies:
-        copy.wait()
+    last.wait()
+
+
+def finish(
+    filtered_far,
+    ratio_far,
+    lev_far,
+    prior_far,
+    limit_far,
+    filtered_out,
+    ratio_out,
+    ph_out,
+    filtered,
+    ratio,
+    lev,
+    prior,
+    limit,
+    ph,
+    temp,
+    load_sem,
+    store_sem,
+):
+    groups = ROWS // GROUP
+    loads = [
+        pltpu.make_async_copy(src, dst, load_sem.at[i])
+        for i, (src, dst) in enumerate(
+            [(prior_far, prior), (limit_far, limit), (filtered_far, filtered), (ratio_far, ratio)]
+            + [(lev_far.at[:, pl.ds(4 * i, 4)], lev.at[:, pl.ds(4 * i, 4)]) for i in range(groups)]
+        )
+    ]
+    for i in (0, 1, 4, 5, 6, 7, 2, 3):
+        loads[i].start()
+    stores = [
+        pltpu.make_async_copy(filtered, filtered_out, store_sem.at[0]),
+        pltpu.make_async_copy(ratio, ratio_out, store_sem.at[1]),
+    ]
+    loads[0].wait()
+    loads[1].wait()
+    for i in range(groups):
+        loads[4 + i].wait()
+        for g in range(GROUP):
+            q = i * GROUP + g
+            base = jnp.broadcast_to(prior[0, q : q + 1, :], (8, LANES))
+            low = jnp.broadcast_to(prior[1, q : q + 1, :], (8, LANES))
+            scale = jnp.broadcast_to(1.0 / limit[q : q + 1, :].astype(F32), (8, LANES))
+            out = []
+            for k in range(8):
+                climb = base + lev[0, q, 8 * k : 8 * k + 8]
+                lowest = jnp.minimum(low, base + lev[1, q, 8 * k : 8 * k + 8])
+                out.append((climb - lowest) * scale)
+            ph[:, q * LANES : (q + 1) * LANES] = in_order(temp, g, out)
+        span = pl.ds(i * GROUP * LANES, GROUP * LANES)
+        stores.append(
+            pltpu.make_async_copy(ph.at[:, span], ph_out.at[:, span], store_sem.at[2 + i])
+        )
+        stores[-1].start()
+        if i < 2:
+            loads[2 + i].wait()
+            stores[i].start()
+    for store in stores:
+        store.wait()
 
 
 def body(nf, nt, strain, fan_cut, sta_len, lta_len, drift_code, threshold):
@@ -695,14 +750,15 @@
         out_shape=(
             jax.ShapeDtypeStruct((HOP, chans), BF16),
             jax.ShapeDtypeStruct((HOP, chans), F32),
-            jax.ShapeDtypeStruct((HOP, chans), F32),
+            jax.ShapeDtypeStruct((2, ROWS, HOP, LANES), F32),
+            jax.ShapeDtypeStruct((2, ROWS, LANES), F32),
         ),
-        in_specs=[far] * 13,
-        out_specs=(far, far, far),
+        in_specs=[far] * 12,
+        out_specs=(far,) * 4,
         scratch_shapes=[
             pltpu.VMEM((HOP, chans), BF16),
             pltpu.SMEM((BINS,), jnp.int32),
-            pltpu.VMEM((4, ROWS, LANES), jnp.int32),
+            pltpu.VMEM((3, ROWS, LANES), jnp.int32),
         ]
         + [pltpu.VMEM(t.shape, F32) for t in tabs]
         + [
@@ -713,17 +769,16 @@
             pltpu.VMEM((FRAME, 3 * FRAME), BF16),
             pltpu.VMEM((HOP, chans), BF16),
             pltpu.VMEM((HOP, chans), F32),
-            pltpu.VMEM((HOP, chans), F32),
             pltpu.VMEM((HOP, chans), BF16),
             pltpu.VMEM((FRAME, ROWS, LANES), F32),
-            pltpu.VMEM((BINS, ROWS, 2 * LANES), i16),
-            pltpu.VMEM((per, rows, 2 * LANES), i16),
-            pltpu.VMEM((1, 1, LANES), F32),
-            pltpu.VMEM((nf, 1, LANES), F32),
+            pltpu.VMEM((2, BINS, ROWS, LANES), i16),
+            pltpu.VMEM((2, nf, per, ROWS, LANES), i16),
+            pltpu.VMEM((2, 1, LANES), F32),
+            pltpu.VMEM((2, nf, 1, LANES), F32),
             pltpu.VMEM((2, 3 * half, 2 * LANES), BF16),
             pltpu.VMEM((2, 3 * half, 2 * LANES), BF16),
-            pltpu.VMEM((per, rows, 2 * LANES), i16),
-            pltpu.VMEM((BINS, ROWS, 2 * LANES), i16),
+            pltpu.VMEM((per, nf, 2, ROWS, LANES), i16),
+            pltpu.VMEM((BINS, 2, ROWS, LANES), i16),
             pltpu.VMEM((per, 2, 1, LANES), F32),
             pltpu.VMEM((BINS, 1, LANES), F32),
             pltpu.VMEM((2, BINS, ROWS, LANES), F32),
@@ -742,12 +797,12 @@
             pltpu.VMEM((GROUP, HOP, LANES), F32),
             dma((4,)),
             dma((4,)),
-            dma((per, nf)),
-            dma((per, nf)),
-            dma((nf,)),
-            dma((nf,)),
-            dma((per, nf)),
-            dma((per, nf)),
+            dma((per + 1, nf)),
+            dma((per + 1, nf)),
+            dma((2, nf)),
+            dma((2, nf)),
+            dma((per + 1, nf)),
+            dma((per + 1, nf)),
             dma((per, nf)),
             dma((per, nf)),
             dma((4,)),
@@ -758,21 +813,35 @@
             dma((nt,)),
             dma((nt,)),
             dma((nt,)),
-            dma((13,)),
-            dma((3,)),
+            dma((12,)),
+            dma((4,)),
         ],
         compiler_params=pltpu.CompilerParams(
             collective_id=0, has_side_effects=True, vmem_limit_bytes=64 * 1024 * 1024
         ),
-    )(strain, fan_cut, *per_chan, *tabs)
+    )(strain, fan_cut, *per_chan[:3], *tabs)
     return pl.pallas_call(
-        hand_over,
-        out_shape=tuple(jax.ShapeDtypeStruct(r.shape, r.dtype) for r in results),
-        in_specs=[far] * 3,
+        finish,
+        out_shape=(
+            jax.ShapeDtypeStruct((HOP, chans), BF16),
+            jax.ShapeDtypeStruct((HOP, chans), F32),
+            jax.ShapeDtypeStruct((HOP, chans), F32),
+        ),
+        in_specs=[far] * 5,
         out_specs=(far,) * 3,
-        scratch_shapes=[dma((3,))],
+        scratch_shapes=[
+            pltpu.VMEM((HOP, chans), BF16),
+            pltpu.VMEM((HOP, chans), F32),
+            pltpu.VMEM((2, ROWS, HOP, LANES), F32),
+            pltpu.VMEM((2, ROWS, LANES), F32),
+            pltpu.VMEM((ROWS, LANES), jnp.int32),
+            pltpu.VMEM((HOP, chans), F32),
+            pltpu.VMEM((GROUP, HOP, LANES), F32),
+            dma((8,)),
+            dma((6,)),
+        ],
         compiler_params=pltpu.CompilerParams(vmem_limit_bytes=64 * 1024 * 1024),
-    )(*results)
+    )(*results, per_chan[3])
 
 
 def solution(mesh):

time: 109 us -> 71.3 us (0.65)
  Pallas kernels: 108 us -> 70.5 us
    pallas_call x1, Pallas kernels: 40.8 us -> 2.46 us  [body(): pl.pallas_call(finish, out_shape=(jax.ShapeDtypeStruct((HOP, chans), BF16...]
where the time goes in v3:
time: 71.3 us; the launch traced here: 71.1 us
  Pallas kernels  70.5 us (99%)
    pallas_call x1, Pallas kernels, body(): pl.pallas_call(functools.partial(kernel, nf, nt), out_shape=(jax.ShapeDty...  68 us
    pallas_call x1, Pallas kernels, body(): pl.pallas_call(finish, out_shape=(jax.ShapeDtypeStruct((HOP, chans), BF16...  2.46 us

profile of v3, /device:TPU:1, one launch (start us, length us, event | category | flops | bytes accessed | tf_op | source)
XLA Modules:
  0.0 71.1 jit_solution(9483019144587183614)
XLA Ops:
  0.6 68.0 %shard_map.148 = (bf16[64,2048]{1,0:T(8,128)(2,1)}, f32[64,2048]{1,0:T(8,128)}, f32[2,16,64,128]{3,2,1,0:T(8,128)}, f32[2,16,128]{2,1,0:T(8,128)}) custom-call(bf16[64,2048]{1,0:T(8,128)(2,1)} %refs_0_.1, s32[64]{0:T(128)} %refs_1_.1, s32[16,128]{1,0:T(8,128)} %bitcast.4, s32[16,128]{1,0:T(8,128)} %bitcast.5, s32[16,128]{1,0:T(8,128)} %bitcast.6, ...), custom_call_target="tpu_custom_call" | custom-call | tf_op jit(solution)/shard_map/pallas_call | solution.py:748
  68.6 2.5 %shard_map.149 = (bf16[64,2048]{1,0:T(8,128)(2,1)}, f32[64,2048]{1,0:T(8,128)}, f32[64,2048]{1,0:T(8,128)}) custom-call(bf16[64,2048]{1,0:T(8,128)(2,1)} %get-tuple-element.7.filtered_far, f32[64,2048]{1,0:T(8,128)} %get-tuple-element.8.ratio_far, f32[2,16,64,128]{3,2,1,0:T(8,128)} %get-tuple-element.9.lev_far, f32[2,16,128]{2,1,0:T(8,128)} %get-tuple-element.10.prior_far, ...), custom_call_target="tpu_custom_call" | custom-call | tf_op jit(solution)/shard_map/pallas_call | solution.py:823

commit v4 on v3

--- a/solution.py
+++ b/solution.py
@@ -28,6 +28,7 @@
 
 def tables(total):
     rows = total // LANES
+    nf = rows // ROWS
     half = rows // 2
     n = np.arange(FRAME)
     f = np.arange(BINS)
@@ -37,7 +38,9 @@
     weight = np.where(f == 0, 1.0, 2.0)[:, None] / FRAME
     synthesis = np.concatenate([weight * np.cos(angle), -weight * np.sin(angle)], 0).T
     order = time_order()
+    arrived = np.arange(BINS).reshape(nf, BINS // nf).T.reshape(-1)
     synthesis = synthesis[np.concatenate([order, HOP + order])]
+    synthesis = synthesis[:, np.concatenate([arrived, BINS + arrived])]
     a = np.arange(half)
     outer = 2.0 * math.pi / half * ((a[:, None] * a[None, :]) % half)
     outer = np.concatenate([np.cos(outer), -np.sin(outer)], 0)
@@ -121,13 +124,16 @@
         rim,
         spec,
         snd1,
-        rcv1,
+        rcva,
+        rcvb,
         scs1,
         scr1,
         x3,
         z3,
-        snd2,
-        rcv2,
+        snde,
+        sndl,
+        rcve,
+        rcvl,
         scs2,
         scr2,
         deco,
@@ -246,25 +252,27 @@
 
     tall = ROWS // 2
 
-    def scale1(h, j):
+    def scale1(j):
         to = lax.rem(me + j, nf)
-        return remote(scs1.at[h], scr1.at[h, me], c1s.at[h, j], c1r.at[h, j], fiber=to)
+        return remote(scs1, scr1.at[me], c1s.at[0], c1r.at[0], fiber=to)
 
     def data1(i, j):
         to = lax.rem(me + j, nf)
         if i == 0:
-            src, dst = snd1.at[0, pl.ds(to * per, per)], rcv1.at[0, me]
+            src, dst = snd1.at[0, pl.ds(to * per, per)], rcva.at[me]
         else:
-            src, dst = snd1.at[1, to * per + i - 1], rcv1.at[1, me, i - 1]
-        return remote(src, dst, s1s.at[i, j], s1r.at[i, j], fiber=to)
-
-    def from1(i, j):
-        back = lax.rem(me + nf - j, nf)
-        if i == 0:
-            src, dst = snd1.at[0, pl.ds(0, per)], rcv1.at[0, back]
-        else:
-            src, dst = snd1.at[1, 0], rcv1.at[1, back, i - 1]
-        return remote(src, dst, s1s.at[i, j], s1r.at[i, j], fiber=back)
+            src, dst = snd1.at[1, to * per + i - 1], rcvb.at[i - 1, me]
+        return remote(src, dst, s1s.at[i], s1r.at[i], fiber=to)
+
+    def of_all(ref, send, recv):
+        return remote(ref, ref, send, recv, fiber=lax.rem(me + 1, nf))
+
+    def all1(i):
+        ref = rcva.at[pl.ds(0, nf - 1)] if i == 0 else rcvb.at[i - 1, pl.ds(0, nf - 1)]
+        return of_all(ref, s1s.at[i], s1r.at[i])
+
+    def all_scales1():
+        return of_all(scr1.at[pl.ds(0, nf - 1)], c1s.at[0], c1r.at[0])
 
     def each_peer(act):
         def one(j, c):
@@ -289,7 +297,7 @@
         peak = peak_of(peak)
         gain = TOP / peak
         scs1[h] = jnp.broadcast_to(peak * (1.0 / TOP), (1, LANES))
-        scr1[h, me] = scs1[h]
+        scr1[me, h] = scs1[h]
 
         def code1(i, c):
             half_rows = slice(h * tall, (h + 1) * tall)
@@ -301,30 +309,22 @@
         lax.fori_loop(0, BINS // 8, code1, 0)
         if h == 0:
 
-            def send0(j):
-                scale1(0, j).start()
-                data1(0, j).start()
-
-            each_peer(send0)
+            each_peer(lambda j: data1(0, j).start())
+            rcva[me] = snd1[0, pl.ds(me * per, per)]
         else:
 
             def send1(j):
-                scale1(1, j).start()
+                scale1(j).start()
                 data1(1, j).start()
 
             each_peer(send1)
             for b in range(1, per):
                 each_peer(lambda j: data1(1 + b, j).start())
-        rcv1[h, me] = snd1[h, pl.ds(me * per, per)]
-
-    def first_scales(j):
-        back = lax.rem(me + nf - j, nf)
-        for h in range(2):
-            remote(
-                scs1.at[h], scr1.at[h, back], c1s.at[h, j], c1r.at[h, j], fiber=back
-            ).wait_recv()
-
-    each_peer(lambda j: from1(0, j).wait_recv())
+            for b in range(per):
+                rcvb[b, me] = snd1[1, me * per + b]
+
+    all1(0).wait_recv()
+    all_scales1().wait_recv()
 
     for load in loads[6:]:
         load.wait()
@@ -332,27 +332,27 @@
 
     final = per - 1
 
-    def scale2(b, j):
+    def scale2(j):
         to = lax.rem(me + j, nf)
-        return remote(
-            scs2.at[b, to // peers], scr2.at[me * per + b], c2s.at[b, j], c2r.at[b, j], fiber=to
-        )
+        return remote(scs2.at[to // peers], scr2.at[me], c2s.at[0], c2r.at[0], fiber=to)
 
     def data2(i, j):
         to = lax.rem(me + j, nf)
         if i < final:
-            src, dst = snd2.at[i, to], rcv2.at[me * per + i]
+            src, dst = snde.at[i, to], rcve.at[i, me]
         else:
-            src, dst = snd2.at[final, to, i - final], rcv2.at[me * per + final, i - final]
-        return remote(src, dst, s2s.at[i, j], s2r.at[i, j], fiber=to)
-
-    def from2(i, j):
-        back = lax.rem(me + nf - j, nf)
+            src, dst = sndl.at[i - final, to], rcvl.at[i - final, me]
+        return remote(src, dst, s2s.at[i], s2r.at[i], fiber=to)
+
+    def all2(i):
         if i < final:
-            src, dst = snd2.at[i, 0], rcv2.at[back * per + i]
+            ref = rcve.at[i, pl.ds(0, nf - 1)]
         else:
-            src, dst = snd2.at[final, 0, 0], rcv2.at[back * per + final, i - final]
-        return remote(src, dst, s2s.at[i, j], s2r.at[i, j], fiber=back)
+            ref = rcvl.at[i - final, pl.ds(0, nf - 1)]
+        return of_all(ref, s2s.at[i], s2r.at[i])
+
+    def all_scales2():
+        return of_all(scr2.at[pl.ds(0, nf - 1)], c2s.at[0], c2r.at[0])
 
     lane = lax.broadcasted_iota(jnp.int32, (half, LANES), 1)
     row = lax.broadcasted_iota(jnp.int32, (half, LANES), 0)
@@ -366,13 +366,11 @@
             ref[e, pl.ds(pl.multiple_of(i * half + at, ROWS), size), :] = part
 
     for b in range(per):
-        if b == 0:
-            each_peer(first_scales)
-        each_peer(lambda j: from1(1 + b, j).wait_recv())
+        all1(1 + b).wait_recv()
         limit_k = cut[me * per + b]
 
         def values(p):
-            pieces = [rcv1[h, p, b].astype(F32) * scr1[h, p] for h in range(2)]
+            pieces = [x.astype(F32) * scr1[p, h] for h, x in enumerate((rcva[p, b], rcvb[b, p]))]
             return jnp.concatenate(
                 [jnp.concatenate([x[i * tall : (i + 1) * tall] for x in pieces], 0) for i in range(2)],
                 axis=1,
@@ -417,45 +415,51 @@
         vr, vi = re * wr + im * wi, im * wr - re * wi
         for blk, (re, im) in enumerate(((ur + vr, ui + vi), (ur - vr, ui - vi))):
             top = peak_of(jnp.maximum(jnp.abs(re), jnp.abs(im)))
-            scs2[b, blk] = jnp.broadcast_to(top * (1.0 / TOP), (1, LANES))
+            scs2[blk, b] = jnp.broadcast_to(top * (1.0 / TOP), (1, LANES))
             re = re.reshape(peers, 2, tall, LANES)
             im = im.reshape(peers, 2, tall, LANES)
             code = coded(jnp.concatenate([re, im], axis=2), TOP / top)
-            snd2[b, blk * peers : (blk + 1) * peers] = code
-
-        def send2(j):
-            scale2(b, j).start()
-            data2(b, j).start()
-
-        each_peer(send2)
-        if b == final:
+            span = slice(blk * peers, (blk + 1) * peers)
+            if b < final:
+                snde[b, span] = code
+            else:
+                sndl[0, span] = code[:, 0]
+                sndl[1, span] = code[:, 1]
+
+        if b < final:
+            each_peer(lambda j: data2(b, j).start())
+            rcve[b, me] = snde[b, me]
+        else:
+
+            def send2(j):
+                scale2(j).start()
+                data2(final, j).start()
+
+            each_peer(send2)
             each_peer(lambda j: data2(per, j).start())
-        scr2[me * per + b] = scs2[b, me // peers]
-        rcv2[me * per + b] = snd2[b, me]
-
-    def second_scales(j):
-        back = lax.rem(me + nf - j, nf)
-        for b in range(per):
-            remote(
-                scs2.at[0, 0], scr2.at[back * per + b], c2s.at[b, j], c2r.at[b, j], fiber=back
-            ).wait_recv()
+            for h in range(2):
+                rcvl[h, me] = sndl[h, me]
+            scr2[me] = scs2[me // peers]
 
     def back_again(h):
         if h == 0:
             for i in range(per):
-                each_peer(lambda j: from2(i, j).wait_recv())
-            each_peer(second_scales)
+                all2(i).wait_recv()
+            all_scales2().wait_recv()
         else:
-            each_peer(lambda j: from2(per, j).wait_recv())
+            all2(per).wait_recv()
 
         def decode2(i, c):
             at = pl.ds(i * 8, 8)
-            x = rcv2[at, h].astype(F32) * scr2[at]
-            deco[0, at, h * tall : (h + 1) * tall] = x[:, :tall]
-            deco[1, at, h * tall : (h + 1) * tall] = x[:, tall:]
+            for b in range(per):
+                x = rcve[b, at, h] if b < final else rcvl[h, at]
+                x = x.astype(F32) * scr2[at, b]
+                to = pl.ds(b * nf + i * 8, 8)
+                deco[0, to, h * tall : (h + 1) * tall] = x[:, :tall]
+                deco[1, to, h * tall : (h + 1) * tall] = x[:, tall:]
             return c
 
-        lax.fori_loop(0, BINS // 8, decode2, 0)
+        lax.fori_loop(0, nf // 8, decode2, 0)
 
     def spill(c):
         span = pl.ds(c * wide, wide)
@@ -649,16 +653,11 @@
     for chunk in range(chunks):
         rim_copy(chunk).wait_send()
 
-    def all_sent(j):
-        for h in range(2):
-            scale1(h, j).wait_send()
-        for b in range(per):
-            scale2(b, j).wait_send()
-        for i in range(per + 1):
-            data1(i, j).wait_send()
-            data2(i, j).wait_send()
-
-    each_peer(all_sent)
+    for i in range(per + 1):
+        all1(i).wait_send()
+        all2(i).wait_send()
+    all_scales1().wait_send()
+    all_scales2().wait_send()
     for chunk in range(chunks):
         spill_scale(chunk).wait_send()
         spill(chunk).wait_send()
@@ -772,15 +771,18 @@
             pltpu.VMEM((HOP, chans), BF16),
             pltpu.VMEM((FRAME, ROWS, LANES), F32),
             pltpu.VMEM((2, BINS, ROWS, LANES), i16),
-            pltpu.VMEM((2, nf, per, ROWS, LANES), i16),
+            pltpu.VMEM((nf, per, ROWS, LANES), i16),
+            pltpu.VMEM((per, nf, ROWS, LANES), i16),
             pltpu.VMEM((2, 1, LANES), F32),
-            pltpu.VMEM((2, nf, 1, LANES), F32),
+            pltpu.VMEM((nf, 2, 1, LANES), F32),
             pltpu.VMEM((2, 3 * half, 2 * LANES), BF16),
             pltpu.VMEM((2, 3 * half, 2 * LANES), BF16),
-            pltpu.VMEM((per, nf, 2, ROWS, LANES), i16),
-            pltpu.VMEM((BINS, 2, ROWS, LANES), i16),
-            pltpu.VMEM((per, 2, 1, LANES), F32),
-            pltpu.VMEM((BINS, 1, LANES), F32),
+            pltpu.VMEM((per - 1, nf, 2, ROWS, LANES), i16),
+            pltpu.VMEM((2, nf, ROWS, LANES), i16),
+            pltpu.VMEM((per - 1, nf, 2, ROWS, LANES), i16),
+            pltpu.VMEM((2, nf, ROWS, LANES), i16),
+            pltpu.VMEM((2, per, 1, LANES), F32),
+            pltpu.VMEM((nf, per, 1, LANES), F32),
             pltpu.VMEM((2, BINS, ROWS, LANES), F32),
             pltpu.VMEM((ROWS, HOP, LANES), F32),
             pltpu.VMEM((ROWS, HOP, LANES), F32),
@@ -797,14 +799,14 @@
             pltpu.VMEM((GROUP, HOP, LANES), F32),
             dma((4,)),
             dma((4,)),
-            dma((per + 1, nf)),
-            dma((per + 1, nf)),
-            dma((2, nf)),
-            dma((2, nf)),
-            dma((per + 1, nf)),
-            dma((per + 1, nf)),
-            dma((per, nf)),
-            dma((per, nf)),
+            dma((per + 1,)),
+            dma((per + 1,)),
+            dma((1,)),
+            dma((1,)),
+            dma((per + 1,)),
+            dma((per + 1,)),
+            dma((1,)),
+            dma((1,)),
             dma((4,)),
             dma((4,)),
             dma((4,)),

time: 71.3 us -> 65.6 us (0.920)
  Pallas kernels: 70.5 us -> 64.8 us
    pallas_call x1, Pallas kernels: 68 us -> 62.3 us  [body(): pl.pallas_call(functools.partial(kernel, nf, nt), out_shape=(jax.ShapeDty...]
where the time goes in v4:
time: 65.6 us; the launch traced here: 65.4 us
  Pallas kernels  64.8 us (99%)
    pallas_call x1, Pallas kernels, body(): pl.pallas_call(functools.partial(kernel, nf, nt), out_shape=(jax.ShapeDty...  62.3 us
    pallas_call x1, Pallas kernels, body(): pl.pallas_call(finish, out_shape=(jax.ShapeDtypeStruct((HOP, chans), BF16...  2.46 us

profile of v4, /device:TPU:1, one launch (start us, length us, event | category | flops | bytes accessed | tf_op | source)
XLA Modules:
  0.0 65.4 jit_solution(13195642257748626550)
XLA Ops:
  0.6 62.3 %shard_map.148 = (bf16[64,2048]{1,0:T(8,128)(2,1)}, f32[64,2048]{1,0:T(8,128)}, f32[2,16,64,128]{3,2,1,0:T(8,128)}, f32[2,16,128]{2,1,0:T(8,128)}) custom-call(bf16[64,2048]{1,0:T(8,128)(2,1)} %refs_0_.1, s32[64]{0:T(128)} %refs_1_.1, s32[16,128]{1,0:T(8,128)} %bitcast.4, s32[16,128]{1,0:T(8,128)} %bitcast.5, s32[16,128]{1,0:T(8,128)} %bitcast.6, ...), custom_call_target="tpu_custom_call" | custom-call | tf_op jit(solution)/shard_map/pallas_call | solution.py:747
  63.0 2.5 %shard_map.149 = (bf16[64,2048]{1,0:T(8,128)(2,1)}, f32[64,2048]{1,0:T(8,128)}, f32[64,2048]{1,0:T(8,128)}) custom-call(bf16[64,2048]{1,0:T(8,128)(2,1)} %get-tuple-element.7.filtered_far, f32[64,2048]{1,0:T(8,128)} %get-tuple-element.8.ratio_far, f32[2,16,64,128]{3,2,1,0:T(8,128)} %get-tuple-element.9.lev_far, f32[2,16,128]{2,1,0:T(8,128)} %get-tuple-element.10.prior_far, ...), custom_call_target="tpu_custom_call" | custom-call | tf_op jit(solution)/shard_map/pallas_call | solution.py:825

commit v5 on v4

--- a/solution.py
+++ b/solution.py
@@ -130,8 +130,7 @@
         scr1,
         x3,
         z3,
-        snde,
-        sndl,
+        snd2,
         rcve,
         rcvl,
         scs2,
@@ -146,9 +145,17 @@
         lev,
         seg,
         cars,
-        carr,
+        carsib,
+        cartot,
+        carall,
+        cargift,
+        start,
         sums,
-        sumr,
+        sumsib,
+        sumtot,
+        sumall,
+        sumgift,
+        prior,
         temp,
         rim_s,
         rim_r,
@@ -164,10 +171,10 @@
         sp_r,
         ss_s,
         ss_r,
-        ca_s,
-        ca_r,
-        su_s,
-        su_r,
+        sib_s,
+        sib_r,
+        z_s,
+        z_r,
         load_sem,
         store_sem,
     ) = refs
@@ -186,20 +193,35 @@
 
     barrier = pltpu.get_barrier_semaphore()
 
-    def greet_fiber(j, c):
-        pl.semaphore_signal(
-            barrier, inc=1, device_id={"fiber": lax.rem(me + j, nf)}, device_id_type=MESH
-        )
-        return c
-
-    def greet_tm(j, c):
-        pl.semaphore_signal(
-            barrier, inc=1, device_id={"tm": lax.rem(tm + j, nt)}, device_id_type=MESH
-        )
-        return c
-
-    lax.fori_loop(1, nt, greet_tm, 0)
-    lax.fori_loop(1, nf, greet_fiber, 0)
+    width = 4
+    lines = nf // width
+
+    def each_peer(act):
+        def one(i, c):
+            g = i // width
+            back = (g + 1) // 2
+            down = lines // 2 + jnp.where(g % 2 == 0, back, -back)
+            over = lax.rem(i, width) + jnp.where(g == lines - 1, 1, 0)
+            act(lax.rem(me // width + down, lines) * width + lax.rem(me + over, width))
+            return c
+
+        lax.fori_loop(0, nf - 1, one, 0)
+
+    def greet(**to):
+        pl.semaphore_signal(barrier, inc=1, device_id=to, device_id_type=MESH)
+
+    nz = nt // 2
+    friends = list(dict.fromkeys((1, nt - 1, *range(2, nt, 2))))
+    for j in friends:
+        greet(tm=lax.rem(tm + j, nt))
+    line = me // width
+    mine = lax.rem(me, width)
+    beside = [lax.rem(mine + i, width) for i in range(width)]
+    for g in range(lines):
+        down = lines // 2 + (g + 1) // 2 * (1 if g % 2 == 0 else -1)
+        at = lax.rem(line + down, lines) * width
+        for i in range(1 if g == lines - 1 else 0, width):
+            greet(fiber=at + beside[i])
 
     loads = [
         pltpu.make_async_copy(src, dst, load_sem.at[i])
@@ -226,7 +248,7 @@
     def rates(i, at):
         return chan[i, at, :].astype(F32)
 
-    pl.semaphore_wait(barrier, nf - 1 + nt - 1)
+    pl.semaphore_wait(barrier, nf - 1 + len(friends))
 
     chunks = 4
     wide = ROWS // chunks
@@ -235,8 +257,10 @@
         span = pl.ds(c * wide * LANES, wide * LANES)
         return remote(strain_far.at[:, span], rim.at[:, span], rim_s.at[c], rim_r.at[c], tm=later)
 
-    for chunk in range(chunks):
-        rim_copy(chunk).start()
+    @pl.when(tm < nt - 1)
+    def _():
+        for chunk in range(chunks):
+            rim_copy(chunk).start()
 
     for load in loads[:6]:
         load.wait()
@@ -252,12 +276,10 @@
 
     tall = ROWS // 2
 
-    def scale1(j):
-        to = lax.rem(me + j, nf)
+    def scale1(to):
         return remote(scs1, scr1.at[me], c1s.at[0], c1r.at[0], fiber=to)
 
-    def data1(i, j):
-        to = lax.rem(me + j, nf)
+    def data1(i, to):
         if i == 0:
             src, dst = snd1.at[0, pl.ds(to * per, per)], rcva.at[me]
         else:
@@ -268,23 +290,16 @@
         return remote(ref, ref, send, recv, fiber=lax.rem(me + 1, nf))
 
     def all1(i):
-        ref = rcva.at[pl.ds(0, nf - 1)] if i == 0 else rcvb.at[i - 1, pl.ds(0, nf - 1)]
+        ref = rcva.at[pl.ds(0, nf - 1)] if isinstance(i, int) and i == 0 else rcvb.at[i - 1, pl.ds(0, nf - 1)]
         return of_all(ref, s1s.at[i], s1r.at[i])
 
     def all_scales1():
         return of_all(scr1.at[pl.ds(0, nf - 1)], c1s.at[0], c1r.at[0])
-
-    def each_peer(act):
-        def one(j, c):
-            act(j)
-            return c
-
-        lax.fori_loop(1, nf, one, 0)
 
     for h in range(2):
         peak = jnp.zeros((1, 2 * LANES), F32)
         for chunk in range(h * chunks // 2, (h + 1) * chunks // 2):
-            rim_copy(chunk).wait_recv()
+            pl.when(tm > 0)(rim_copy(chunk).wait_recv)
             for q in range(chunk * wide, (chunk + 1) * wide, 2):
                 cols = slice(q * LANES, (q + 2) * LANES)
                 before = jnp.where(tm > 0, rim[:, cols].astype(F32), 0.0).astype(BF16)
@@ -299,17 +314,12 @@
         scs1[h] = jnp.broadcast_to(peak * (1.0 / TOP), (1, LANES))
         scr1[me, h] = scs1[h]
 
-        def code1(i, c):
-            half_rows = slice(h * tall, (h + 1) * tall)
-            re = spec[pl.ds(i * 8, 8), half_rows, :]
-            im = spec[pl.ds(BINS + i * 8, 8), half_rows, :]
-            snd1[h, pl.ds(i * 8, 8)] = coded(jnp.concatenate([re, im], axis=1), gain)
-            return c
-
-        lax.fori_loop(0, BINS // 8, code1, 0)
+        half_rows = slice(h * tall, (h + 1) * tall)
+        re, im = spec[:BINS, half_rows, :], spec[BINS:, half_rows, :]
+        snd1[h] = coded(jnp.concatenate([re, im], axis=1), gain)
         if h == 0:
 
-            each_peer(lambda j: data1(0, j).start())
+            each_peer(lambda to: data1(0, to).start())
             rcva[me] = snd1[0, pl.ds(me * per, per)]
         else:
 
@@ -319,7 +329,7 @@
 
             each_peer(send1)
             for b in range(1, per):
-                each_peer(lambda j: data1(1 + b, j).start())
+                each_peer(lambda to: data1(1 + b, to).start())
             for b in range(per):
                 rcvb[b, me] = snd1[1, me * per + b]
 
@@ -332,17 +342,15 @@
 
     final = per - 1
 
-    def scale2(j):
-        to = lax.rem(me + j, nf)
+    def scale2(to):
         return remote(scs2.at[to // peers], scr2.at[me], c2s.at[0], c2r.at[0], fiber=to)
 
-    def data2(i, j):
-        to = lax.rem(me + j, nf)
-        if i < final:
-            src, dst = snde.at[i, to], rcve.at[i, me]
-        else:
-            src, dst = sndl.at[i - final, to], rcvl.at[i - final, me]
-        return remote(src, dst, s2s.at[i], s2r.at[i], fiber=to)
+    def early2(b, to):
+        return remote(snd2.at[b, to], rcve.at[b, me], s2s.at[b], s2r.at[b], fiber=to)
+
+    def last2(h, to):
+        i = final + h
+        return remote(snd2.at[final, to, h], rcvl.at[h, me], s2s.at[i], s2r.at[i], fiber=to)
 
     def all2(i):
         if i < final:
@@ -365,7 +373,7 @@
         for i, part in enumerate((high, low, high)):
             ref[e, pl.ds(pl.multiple_of(i * half + at, ROWS), size), :] = part
 
-    for b in range(per):
+    def transform(b):
         all1(1 + b).wait_recv()
         limit_k = cut[me * per + b]
 
@@ -390,12 +398,12 @@
 
         lax.fori_loop(0, peers // GROUP, decode, 0)
 
-        for e in range(2):
+        def waves(e, c):
             pq = jnp.dot(outer[...], x3[e], preferred_element_type=F32)
             pr, pi = parts(pq[:half])
             qr, qi = parts(pq[half:])
             re, im = pr - qi, pi + qr
-            tr, ti = parts(turn[e * half : (e + 1) * half, :])
+            tr, ti = parts(turn[pl.ds(pl.multiple_of(e * half, half), half), :])
             y = jnp.concatenate([re * tr - im * ti, re * ti + im * tr], axis=1)
             wr, wi = parts(jnp.dot(across(y), fwd[...], preferred_element_type=F32))
             k = 2 * row + e + rows * lane
@@ -403,6 +411,9 @@
             w = jnp.concatenate([jnp.where(keep, wr, 0.0), jnp.where(keep, wi, 0.0)], axis=1)
             re, im = parts(jnp.dot(across(w), inv[...], preferred_element_type=F32))
             put(z3, e, 0, half, jnp.concatenate([re * tr + im * ti, im * tr - re * ti], axis=1))
+            return c
+
+        lax.fori_loop(0, 2, waves, 0)
 
         back = []
         for e in range(2):
@@ -420,26 +431,30 @@
             im = im.reshape(peers, 2, tall, LANES)
             code = coded(jnp.concatenate([re, im], axis=2), TOP / top)
             span = slice(blk * peers, (blk + 1) * peers)
-            if b < final:
-                snde[b, span] = code
-            else:
-                sndl[0, span] = code[:, 0]
-                sndl[1, span] = code[:, 1]
-
-        if b < final:
-            each_peer(lambda j: data2(b, j).start())
-            rcve[b, me] = snde[b, me]
-        else:
-
-            def send2(j):
-                scale2(j).start()
-                data2(final, j).start()
-
-            each_peer(send2)
-            each_peer(lambda j: data2(per, j).start())
-            for h in range(2):
-                rcvl[h, me] = sndl[h, me]
-            scr2[me] = scs2[me // peers]
+            snd2[b, span] = code
+
+    def bin_step(b, c):
+        transform(b)
+
+        @pl.when(b < final)
+        def _():
+            each_peer(lambda to: early2(b, to).start())
+
+        return c
+
+    lax.fori_loop(0, per, bin_step, 0)
+
+    def send2(to):
+        scale2(to).start()
+        last2(0, to).start()
+
+    each_peer(send2)
+    each_peer(lambda to: last2(1, to).start())
+    for b in range(final):
+        rcve[b, me] = snd2[b, me]
+    for h in range(2):
+        rcvl[h, me] = snd2[final, me, h]
+    scr2[me] = scs2[me // peers]
 
     def back_again(h):
         if h == 0:
@@ -449,17 +464,12 @@
         else:
             all2(per).wait_recv()
 
-        def decode2(i, c):
-            at = pl.ds(i * 8, 8)
-            for b in range(per):
-                x = rcve[b, at, h] if b < final else rcvl[h, at]
-                x = x.astype(F32) * scr2[at, b]
-                to = pl.ds(b * nf + i * 8, 8)
-                deco[0, to, h * tall : (h + 1) * tall] = x[:, :tall]
-                deco[1, to, h * tall : (h + 1) * tall] = x[:, tall:]
-            return c
-
-        lax.fori_loop(0, nf // 8, decode2, 0)
+        for b in range(per):
+            x = rcve[b, :, h] if b < final else rcvl[h]
+            x = x.astype(F32) * scr2[:, b]
+            to = slice(b * nf, (b + 1) * nf)
+            deco[0, to, h * tall : (h + 1) * tall] = x[:, :tall]
+            deco[1, to, h * tall : (h + 1) * tall] = x[:, tall:]
 
     def spill(c):
         span = pl.ds(c * wide, wide)
@@ -489,12 +499,11 @@
                 tail[q + i] = got[HOP:, i * LANES : (i + 1) * LANES]
             top = jnp.maximum(top, peak_of(got[:HOP]))
         sss[chunk] = jnp.broadcast_to(top * (1.0 / TOP), (1, LANES))
-        spill_scale(chunk).start()
+        pl.when(tm > 0)(spill_scale(chunk).start)
         for q in range(chunk * wide, (chunk + 1) * wide):
             sps[q] = coded(head[q], TOP / top)
-        spill(chunk).start()
-
-    has_next = jnp.where(tm < nt - 1, 1.0, 0.0).astype(F32)
+        pl.when(tm > 0)(spill(chunk).start)
+
     seg_id = lax.broadcasted_iota(jnp.int32, (8, LANES), 0)
 
     def shifted(x, by, fill):
@@ -506,22 +515,16 @@
     def natural(g, vectors):
         return in_order(temp, g, vectors)
 
-    def grouped(one):
-        def group(i, c):
-            for g in range(GROUP):
-                one(i * GROUP + g, g)
-            return c
-
-        return group
-
-    for chunk in range(chunks):
-        spill_scale(chunk).wait_recv()
-        spill(chunk).wait_recv()
+    def scan_chunk(chunk, c):
+        @pl.when(tm < nt - 1)
+        def _():
+            spill_scale(chunk).wait_recv()
+            spill(chunk).wait_recv()
 
         def scan_row(q, g):
             at = pl.ds(q, 1)
             cols = pl.ds(pl.multiple_of(q * LANES, LANES), LANES)
-            heads = spr[q].astype(F32) * (ssr[chunk] * has_next)
+            heads = jnp.where(tm < nt - 1, spr[q].astype(F32) * ssr[chunk], 0.0)
             rounded = (tail[q] + heads).astype(BF16).astype(F32)
             part = [rounded[8 * i : 8 * i + 8] for i in range(8)]
             filtered[:, cols] = natural(g, part).astype(BF16)
@@ -541,10 +544,13 @@
                     level = level + power * shifted(level, by, 0.0)
                     power = power * power
                 seg[s, q] = shifted(level, 1, 0.0)
-                cars[s, at, :] = level[7:8]
+                cars[q // tall, s, pl.ds(lax.rem(q, tall), 1), :] = level[7:8]
 
         for g in range(wide):
             scan_row(chunk * wide + g, g)
+        return c
+
+    lax.fori_loop(0, chunks, scan_chunk, 0)
 
     stores = [
         pltpu.make_async_copy(src, dst, store_sem.at[i])
@@ -552,49 +558,87 @@
     ]
     stores[0].start()
 
-    def to_later(snd, rcv, send, recv, j):
-        return remote(snd, rcv.at[tm], send.at[j], recv.at[j], tm=lax.rem(tm + j, nt))
-
-    def from_earlier(snd, rcv, send, recv, j):
-        back = lax.rem(tm + nt - j, nt)
-        return remote(snd, rcv.at[back], send.at[j], recv.at[j], tm=back)
-
-    def pass_on(snd, rcv, send, recv):
+    core = lax.rem(tm, 2)
+    chip = tm // 2
+    sibling = tm + 1 - 2 * core
+
+    def give(src, dst, i):
+        return remote(src, dst, sib_s.at[i], sib_r.at[i], tm=sibling)
+
+    def to_later(snd, rcv, i, j):
+        to = lax.rem(tm + 2 * j, nt)
+        return remote(snd, rcv.at[chip], z_s.at[i, j], z_r.at[i, j], tm=to)
+
+    def from_earlier(snd, rcv, i, j):
+        back = lax.rem(tm + nt - 2 * j, nt)
+        return remote(snd, rcv.at[chip - j], z_s.at[i, j], z_r.at[i, j], tm=back)
+
+    def pair_of(ref):
+        return ref[0], ref[1]
+
+    def chosen(first, second):
+        return tuple(jnp.where(core == 0, a, b) for a, b in zip(first, second))
+
+    def pass_on(i, own, sib, tot, totr, gift, entry, join, apply, step, begin):
+        half_away = give(own.at[1 - core], sib, 2 * i)
+        half_away.start()
+        half_away.wait_recv()
+        mine, other = pair_of(own.at[core]), pair_of(sib)
+        early, late = chosen(mine, other), chosen(other, mine)
+        tot[0], tot[1] = join(early, late)
+
         def out(j, c):
-            to_later(snd, rcv, send, recv, j).start()
+            to_later(tot, totr, i, j).start()
             return c
 
-        lax.fori_loop(1, nt - tm, out, 0)
+        lax.fori_loop(1, nz - chip, out, 0)
 
         def come(j, c):
-            from_earlier(snd, rcv, send, recv, j).wait_recv()
+            from_earlier(tot, totr, i, j).wait_recv()
             return c
 
-        lax.fori_loop(1, tm + 1, come, 0)
-
-    pass_on(cars, carr, ca_s, ca_r)
+        lax.fori_loop(1, chip + 1, come, 0)
+        state = lax.fori_loop(0, chip, lambda k, state: apply(state, pair_of(totr.at[k])), begin)
+        after = step(state, early)
+        entry[core, 0], entry[core, 1] = chosen(state, after)
+        gift[0], gift[1] = chosen(after, state)
+        give(gift, entry.at[core], 2 * i + 1).start()
+
+    my_rows = pl.ds(pl.multiple_of(core * tall, tall), tall)
     decay = []
     for s in range(2):
-        power = rate_of(chan[s].astype(F32))
+        power = rate_of(chan[s, my_rows, :].astype(F32))
         for _ in range(6):
             power = power * power
         decay.append(power)
 
-    def lap(k, state):
-        return tuple(decay[s] * state[s] + carr[k, s] for s in range(2))
-
-    ones = jnp.ones((ROWS, LANES), F32)
-    start = lax.fori_loop(0, tm, lap, (ones, ones))
-    head[0, 0:ROWS] = start[0]
-    head[1, 0:ROWS] = start[1]
-
-    def climb_row(q, g):
+    def later_by(times, state, more):
+        return tuple(g**times * x + y for g, x, y in zip(decay, state, more))
+
+    ones = jnp.ones((tall, LANES), F32)
+    pass_on(
+        0,
+        cars,
+        carsib,
+        cartot,
+        carall,
+        cargift,
+        start,
+        functools.partial(later_by, 1),
+        functools.partial(later_by, 2),
+        functools.partial(later_by, 1),
+        (ones, ones),
+    )
+
+    def climb_row(h, r, g):
+        q = h * tall + r
         at = pl.ds(q, 1)
+        here = pl.ds(r, 1)
         cols = pl.ds(pl.multiple_of(q * LANES, LANES), LANES)
         avg = []
         for s in range(2):
             keep = jnp.broadcast_to(rate_of(rates(s, at)), (8, LANES))
-            carry = jnp.broadcast_to(head[s, at, :], (8, LANES))
+            carry = jnp.broadcast_to(start[h, s, here, :], (8, LANES))
             power = keep * keep
             power = power * power
             power = power * power
@@ -630,44 +674,66 @@
             up = base + climbs[i]
             lev[0, q, 8 * i : 8 * i + 8] = up
             lev[1, q, 8 * i : 8 * i + 8] = jnp.minimum(floor, base + lows[i])
-        sums[0, at, :] = whole[7:8]
-        sums[1, at, :] = least[7:8]
-
-    lax.fori_loop(0, ROWS // GROUP, grouped(climb_row), 0)
+        sums[h, 0, here, :] = whole[7:8]
+        sums[h, 1, here, :] = least[7:8]
+
+    def climb_group(i, c):
+        second = i * GROUP // tall
+
+        @pl.when(i * GROUP == tall)
+        def _():
+            give(cargift, start.at[1 - core], 1).wait_recv()
+
+        h = jnp.where(second == 0, core, 1 - core)
+        for g in range(GROUP):
+            climb_row(h, i * GROUP - second * tall + g, g)
+        return c
+
+    lax.fori_loop(0, ROWS // GROUP, climb_group, 0)
 
     stores[1].start()
     stores[2].start()
-    pass_on(sums, sumr, su_s, su_r)
-
-    def lap2(k, state):
-        total_up, low = state
-        return total_up + sumr[k, 0], jnp.minimum(low, total_up + sumr[k, 1])
-
-    zeros = jnp.zeros((ROWS, LANES), F32)
-    before, low = lax.fori_loop(0, tm, lap2, (zeros, zeros))
-    head[2, 0:ROWS] = before
-    head[3, 0:ROWS] = low
-    last = pltpu.make_async_copy(head.at[pl.ds(2, 2), pl.ds(0, ROWS), :], prior_far, store_sem.at[3])
+
+    def add_up(state, more):
+        return state[0] + more[0], jnp.minimum(state[1], state[0] + more[1])
+
+    zeros = jnp.zeros((tall, LANES), F32)
+    pass_on(
+        1, sums, sumsib, sumtot, sumall, sumgift, prior, add_up, add_up, add_up, (zeros, zeros)
+    )
+    give(sumgift, prior.at[1 - core], 3).wait_recv()
+    last = pltpu.make_async_copy(prior, prior_far, store_sem.at[3])
     last.start()
 
-    for chunk in range(chunks):
-        rim_copy(chunk).wait_send()
+    @pl.when(tm < nt - 1)
+    def _():
+        for chunk in range(chunks):
+            rim_copy(chunk).wait_send()
 
     for i in range(per + 1):
         all1(i).wait_send()
+    for i in range(per + 1):
         all2(i).wait_send()
     all_scales1().wait_send()
     all_scales2().wait_send()
-    for chunk in range(chunks):
-        spill_scale(chunk).wait_send()
-        spill(chunk).wait_send()
+    @pl.when(tm > 0)
+    def _():
+        for chunk in range(chunks):
+            spill_scale(chunk).wait_send()
+            spill(chunk).wait_send()
+
+    for i, (own, sib, gift, entry) in enumerate(
+        ((cars, carsib, cargift, start), (sums, sumsib, sumgift, prior))
+    ):
+        give(own.at[1 - core], sib, 2 * i).wait_send()
+        give(gift, entry.at[core], 2 * i + 1).wait_send()
 
     def sent_on(j, c):
-        to_later(sums, carr, ca_s, ca_r, j).wait_send()
-        to_later(sums, sumr, su_s, su_r, j).wait_send()
+        to_later(cartot, carall, 0, j).wait_send()
+        to_later(sumtot, sumall, 1, j).wait_send()
         return c
 
-    lax.fori_loop(1, nt - tm, sent_on, 0)
+    lax.fori_loop(1, nz - chip, sent_on, 0)
     for store in stores:
         store.wait()
     last.wait()
@@ -712,8 +778,9 @@
         loads[4 + i].wait()
         for g in range(GROUP):
             q = i * GROUP + g
-            base = jnp.broadcast_to(prior[0, q : q + 1, :], (8, LANES))
-            low = jnp.broadcast_to(prior[1, q : q + 1, :], (8, LANES))
+            h, r = divmod(q, ROWS // 2)
+            base = jnp.broadcast_to(prior[h, 0, r : r + 1, :], (8, LANES))
+            low = jnp.broadcast_to(prior[h, 1, r : r + 1, :], (8, LANES))
             scale = jnp.broadcast_to(1.0 / limit[q : q + 1, :].astype(F32), (8, LANES))
             out = []
             for k in range(8):
@@ -750,7 +817,7 @@
             jax.ShapeDtypeStruct((HOP, chans), BF16),
             jax.ShapeDtypeStruct((HOP, chans), F32),
             jax.ShapeDtypeStruct((2, ROWS, HOP, LANES), F32),
-            jax.ShapeDtypeStruct((2, ROWS, LANES), F32),
+            jax.ShapeDtypeStruct((2, 2, ROWS // 2, LANES), F32),
         ),
         in_specs=[far] * 12,
         out_specs=(far,) * 4,
@@ -777,8 +844,7 @@
             pltpu.VMEM((nf, 2, 1, LANES), F32),
             pltpu.VMEM((2, 3 * half, 2 * LANES), BF16),
             pltpu.VMEM((2, 3 * half, 2 * LANES), BF16),
-            pltpu.VMEM((per - 1, nf, 2, ROWS, LANES), i16),
-            pltpu.VMEM((2, nf, ROWS, LANES), i16),
+            pltpu.VMEM((per, nf, 2, ROWS, LANES), i16),
             pltpu.VMEM((per - 1, nf, 2, ROWS, LANES), i16),
             pltpu.VMEM((2, nf, ROWS, LANES), i16),
             pltpu.VMEM((2, per, 1, LANES), F32),
@@ -792,10 +858,17 @@
             pltpu.VMEM((4, 1, LANES), F32),
             pltpu.VMEM((2, ROWS, HOP, LANES), F32),
             pltpu.VMEM((2, ROWS, 8, LANES), F32),
-            pltpu.VMEM((2, ROWS, LANES), F32),
-            pltpu.VMEM((nt, 2, ROWS, LANES), F32),
-            pltpu.VMEM((2, ROWS, LANES), F32),
-            pltpu.VMEM((nt, 2, ROWS, LANES), F32),
+        ]
+        + 2
+        * [
+            pltpu.VMEM((2, 2, ROWS // 2, LANES), F32),
+            pltpu.VMEM((2, ROWS // 2, LANES), F32),
+            pltpu.VMEM((2, ROWS // 2, LANES), F32),
+            pltpu.VMEM((nt // 2, 2, ROWS // 2, LANES), F32),
+            pltpu.VMEM((2, ROWS // 2, LANES), F32),
+            pltpu.VMEM((2, 2, ROWS // 2, LANES), F32),
+        ]
+        + [
             pltpu.VMEM((GROUP, HOP, LANES), F32),
             dma((4,)),
             dma((4,)),
@@ -811,10 +884,10 @@
             dma((4,)),
             dma((4,)),
             dma((4,)),
-            dma((nt,)),
-            dma((nt,)),
-            dma((nt,)),
-            dma((nt,)),
+            dma((4,)),
+            dma((4,)),
+            dma((2, nt // 2)),
+            dma((2, nt // 2)),
             dma((12,)),
             dma((4,)),
         ],
@@ -835,7 +908,7 @@
             pltpu.VMEM((HOP, chans), BF16),
             pltpu.VMEM((HOP, chans), F32),
             pltpu.VMEM((2, ROWS, HOP, LANES), F32),
-            pltpu.VMEM((2, ROWS, LANES), F32),
+            pltpu.VMEM((2, 2, ROWS // 2, LANES), F32),
             pltpu.VMEM((ROWS, LANES), jnp.int32),
             pltpu.VMEM((HOP, chans), F32),
             pltpu.VMEM((GROUP, HOP, LANES), F32),

time: 65.6 us -> 62.9 us (0.959)
  the two profiles are of different devices: /device:TPU:1 before, /device:TPU:137 now
where the time goes in v5:
time: 62.9 us; the launch traced here: 62.7 us
  Pallas kernels  62 us (99%)
  between operations  0.64 us (1%)
    pallas_call x1, Pallas kernels, body(): pl.pallas_call(functools.partial(kernel, nf, nt), out_shape=(jax.ShapeDty...  59.6 us
    pallas_call x1, Pallas kernels, body(): pl.pallas_call(finish, out_shape=(jax.ShapeDtypeStruct((HOP, chans), BF16...  2.46 us

profile of v5, /device:TPU:137, one launch (start us, length us, event | category | flops | bytes accessed | tf_op | source)
XLA Modules:
  0.0 62.7 jit_solution(15404018257030032857)
XLA Ops:
  0.6 59.6 %shard_map.148 = (bf16[64,2048]{1,0:T(8,128)(2,1)}, f32[64,2048]{1,0:T(8,128)}, f32[2,16,64,128]{3,2,1,0:T(8,128)}, f32[2,2,8,128]{3,2,1,0:T(8,128)}) custom-call(bf16[64,2048]{1,0:T(8,128)(2,1)} %refs_0_.1, s32[64]{0:T(128)} %refs_1_.1, s32[16,128]{1,0:T(8,128)} %bitcast.4, s32[16,128]{1,0:T(8,128)} %bitcast.5, s32[16,128]{1,0:T(8,128)} %bitcast.6, ...), custom_call_target="tpu_custom_call" | custom-call | tf_op jit(solution)/shard_map/pallas_call | solution.py:814
  60.2 2.5 %shard_map.149 = (bf16[64,2048]{1,0:T(8,128)(2,1)}, f32[64,2048]{1,0:T(8,128)}, f32[64,2048]{1,0:T(8,128)}) custom-call(bf16[64,2048]{1,0:T(8,128)(2,1)} %get-tuple-element.7.filtered_far, f32[64,2048]{1,0:T(8,128)} %get-tuple-element.8.ratio_far, f32[2,16,64,128]{3,2,1,0:T(8,128)} %get-tuple-element.9.lev_far, ...), custom_call_target="tpu_custom_call" | custom-call | tf_op jit(solution)/shard_map/pallas_call | solution.py:898

commit v6 on v5

--- a/solution.py
+++ b/solution.py
@@ -124,8 +124,7 @@
         rim,
         spec,
         snd1,
-        rcva,
-        rcvb,
+        rcv1,
         scs1,
         scr1,
         x3,
@@ -196,16 +195,22 @@
     width = 4
     lines = nf // width
 
+    line = me // width
+    mine = lax.rem(me, width)
+    beside = [lax.rem(mine + i, width) for i in range(width)]
+
     def each_peer(act):
-        def one(i, c):
-            g = i // width
+        def four(g, c):
             back = (g + 1) // 2
             down = lines // 2 + jnp.where(g % 2 == 0, back, -back)
-            over = lax.rem(i, width) + jnp.where(g == lines - 1, 1, 0)
-            act(lax.rem(me // width + down, lines) * width + lax.rem(me + over, width))
+            at = lax.rem(line + down, lines) * width
+            for i in range(width):
+                act(at + beside[i])
             return c
 
-        lax.fori_loop(0, nf - 1, one, 0)
+        lax.fori_loop(0, lines - 1, four, 0)
+        for i in range(1, width):
+            act(me - mine + beside[i])
 
     def greet(**to):
         pl.semaphore_signal(barrier, inc=1, device_id=to, device_id_type=MESH)
@@ -214,9 +219,6 @@
     friends = list(dict.fromkeys((1, nt - 1, *range(2, nt, 2))))
     for j in friends:
         greet(tm=lax.rem(tm + j, nt))
-    line = me // width
-    mine = lax.rem(me, width)
-    beside = [lax.rem(mine + i, width) for i in range(width)]
     for g in range(lines):
         down = lines // 2 + (g + 1) // 2 * (1 if g % 2 == 0 else -1)
         at = lax.rem(line + down, lines) * width
@@ -280,17 +282,20 @@
         return remote(scs1, scr1.at[me], c1s.at[0], c1r.at[0], fiber=to)
 
     def data1(i, to):
-        if i == 0:
-            src, dst = snd1.at[0, pl.ds(to * per, per)], rcva.at[me]
+        if i < 2:
+            src, dst = snd1.at[to * per, i], rcv1.at[0, me, i]
         else:
-            src, dst = snd1.at[1, to * per + i - 1], rcvb.at[i - 1, me]
+            src, dst = snd1.at[to * per + i - 1], rcv1.at[i - 1, me]
         return remote(src, dst, s1s.at[i], s1r.at[i], fiber=to)
 
     def of_all(ref, send, recv):
         return remote(ref, ref, send, recv, fiber=lax.rem(me + 1, nf))
 
     def all1(i):
-        ref = rcva.at[pl.ds(0, nf - 1)] if isinstance(i, int) and i == 0 else rcvb.at[i - 1, pl.ds(0, nf - 1)]
+        if isinstance(i, int) and i < 2:
+            ref = rcv1.at[0, pl.ds(0, nf - 1), i]
+        else:
+            ref = rcv1.at[i - 1, pl.ds(0, nf - 1)]
         return of_all(ref, s1s.at[i], s1r.at[i])
 
     def all_scales1():
@@ -316,11 +321,10 @@
 
         half_rows = slice(h * tall, (h + 1) * tall)
         re, im = spec[:BINS, half_rows, :], spec[BINS:, half_rows, :]
-        snd1[h] = coded(jnp.concatenate([re, im], axis=1), gain)
+        snd1[:, h] = coded(jnp.concatenate([re, im], axis=1), gain)
         if h == 0:
 
             each_peer(lambda to: data1(0, to).start())
-            rcva[me] = snd1[0, pl.ds(me * per, per)]
         else:
 
             def send1(j):
@@ -331,9 +335,10 @@
             for b in range(1, per):
                 each_peer(lambda to: data1(1 + b, to).start())
             for b in range(per):
-                rcvb[b, me] = snd1[1, me * per + b]
+                rcv1[b, me] = snd1[me * per + b]
 
     all1(0).wait_recv()
+    all1(1).wait_recv()
     all_scales1().wait_recv()
 
     for load in loads[6:]:
@@ -371,32 +376,27 @@
     def put(ref, e, at, size, x):
         high, low = split(x)
         for i, part in enumerate((high, low, high)):
-            ref[e, pl.ds(pl.multiple_of(i * half + at, ROWS), size), :] = part
+            ref[e, i * half + at : i * half + at + size, :] = part
 
     def transform(b):
-        all1(1 + b).wait_recv()
+        pl.when(b > 0)(all1(1 + b).wait_recv)
         limit_k = cut[me * per + b]
 
         def values(p):
-            pieces = [x.astype(F32) * scr1[p, h] for h, x in enumerate((rcva[p, b], rcvb[b, p]))]
+            pieces = [rcv1[b, p, h].astype(F32) * scr1[p, h] for h in range(2)]
             return jnp.concatenate(
                 [jnp.concatenate([x[i * tall : (i + 1) * tall] for x in pieces], 0) for i in range(2)],
                 axis=1,
             )
 
-        def decode(g, c):
-            for i in range(GROUP):
-                p = g * GROUP + i
-                at = pl.multiple_of(p * ROWS, ROWS)
-                early, late = values(p), values(p + peers)
-                wr, wi = parts(step[pl.ds(at, ROWS), :])
-                put(x3, 0, at, ROWS, early + late)
-                re, im = parts(early - late)
-                x = jnp.concatenate([re * wr - im * wi, re * wi + im * wr], axis=1)
-                put(x3, 1, at, ROWS, x)
-            return c
-
-        lax.fori_loop(0, peers // GROUP, decode, 0)
+        for p in range(peers):
+            at = p * ROWS
+            early, late = values(p), values(p + peers)
+            wr, wi = parts(step[at : at + ROWS, :])
+            put(x3, 0, at, ROWS, early + late)
+            re, im = parts(early - late)
+            x = jnp.concatenate([re * wr - im * wi, re * wi + im * wr], axis=1)
+            put(x3, 1, at, ROWS, x)
 
         def waves(e, c):
             pq = jnp.dot(outer[...], x3[e], preferred_element_type=F32)
@@ -499,10 +499,14 @@
                 tail[q + i] = got[HOP:, i * LANES : (i + 1) * LANES]
             top = jnp.maximum(top, peak_of(got[:HOP]))
         sss[chunk] = jnp.broadcast_to(top * (1.0 / TOP), (1, LANES))
-        pl.when(tm > 0)(spill_scale(chunk).start)
         for q in range(chunk * wide, (chunk + 1) * wide):
             sps[q] = coded(head[q], TOP / top)
-        pl.when(tm > 0)(spill(chunk).start)
+
+        @pl.when(tm > 0)
+        def _():
+            spill_scale(chunk).start()
+            spill(chunk).start()
+
 
     seg_id = lax.broadcasted_iota(jnp.int32, (8, LANES), 0)
 
@@ -515,7 +519,7 @@
     def natural(g, vectors):
         return in_order(temp, g, vectors)
 
-    def scan_chunk(chunk, c):
+    for chunk in range(chunks):
         @pl.when(tm < nt - 1)
         def _():
             spill_scale(chunk).wait_recv()
@@ -523,7 +527,7 @@
 
         def scan_row(q, g):
             at = pl.ds(q, 1)
-            cols = pl.ds(pl.multiple_of(q * LANES, LANES), LANES)
+            cols = slice(q * LANES, (q + 1) * LANES)
             heads = jnp.where(tm < nt - 1, spr[q].astype(F32) * ssr[chunk], 0.0)
             rounded = (tail[q] + heads).astype(BF16).astype(F32)
             part = [rounded[8 * i : 8 * i + 8] for i in range(8)]
@@ -544,13 +548,10 @@
                     level = level + power * shifted(level, by, 0.0)
                     power = power * power
                 seg[s, q] = shifted(level, 1, 0.0)
-                cars[q // tall, s, pl.ds(lax.rem(q, tall), 1), :] = level[7:8]
+                cars[q // tall, s, q % tall : q % tall + 1, :] = level[7:8]
 
         for g in range(wide):
             scan_row(chunk * wide + g, g)
-        return c
-
-    lax.fori_loop(0, chunks, scan_chunk, 0)
 
     stores = [
         pltpu.make_async_copy(src, dst, store_sem.at[i])
@@ -630,10 +631,11 @@
         (ones, ones),
     )
 
-    def climb_row(h, r, g):
+    def climb_row(h, r):
         q = h * tall + r
+        g = r % GROUP
         at = pl.ds(q, 1)
-        here = pl.ds(r, 1)
+        here = slice(r, r + 1)
         cols = pl.ds(pl.multiple_of(q * LANES, LANES), LANES)
         avg = []
         for s in range(2):
@@ -677,19 +679,11 @@
         sums[h, 0, here, :] = whole[7:8]
         sums[h, 1, here, :] = least[7:8]
 
-    def climb_group(i, c):
-        second = i * GROUP // tall
-
-        @pl.when(i * GROUP == tall)
-        def _():
-            give(cargift, start.at[1 - core], 1).wait_recv()
-
-        h = jnp.where(second == 0, core, 1 - core)
-        for g in range(GROUP):
-            climb_row(h, i * GROUP - second * tall + g, g)
-        return c
-
-    lax.fori_loop(0, ROWS // GROUP, climb_group, 0)
+    for r in range(tall):
+        climb_row(core, r)
+    give(cargift, start.at[1 - core], 1).wait_recv()
+    for r in range(tall):
+        climb_row(1 - core, r)
 
     stores[1].start()
     stores[2].start()
@@ -837,9 +831,8 @@
             pltpu.VMEM((HOP, chans), F32),
             pltpu.VMEM((HOP, chans), BF16),
             pltpu.VMEM((FRAME, ROWS, LANES), F32),
-            pltpu.VMEM((2, BINS, ROWS, LANES), i16),
-            pltpu.VMEM((nf, per, ROWS, LANES), i16),
-            pltpu.VMEM((per, nf, ROWS, LANES), i16),
+            pltpu.VMEM((BINS, 2, ROWS, LANES), i16),
+            pltpu.VMEM((per, nf, 2, ROWS, LANES), i16),
             pltpu.VMEM((2, 1, LANES), F32),
             pltpu.VMEM((nf, 2, 1, LANES), F32),
             pltpu.VMEM((2, 3 * half, 2 * LANES), BF16),

time: 62.9 us -> 61 us (0.970)
  the two profiles are of different devices: /device:TPU:137 before, /device:TPU:129 now
where the time goes in v6:
time: 61 us; the launch traced here: 60.8 us
  Pallas kernels  60.2 us (99%)
  between operations  0.64 us (1%)
    pallas_call x1, Pallas kernels, body(): pl.pallas_call(functools.partial(kernel, nf, nt), out_shape=(jax.ShapeDty...  57.7 us
    pallas_call x1, Pallas kernels, body(): pl.pallas_call(finish, out_shape=(jax.ShapeDtypeStruct((HOP, chans), BF16...  2.46 us

profile of v6, /device:TPU:129, one launch (start us, length us, event | category | flops | bytes accessed | tf_op | source)
XLA Modules:
  0.0 60.8 jit_solution(11026517389402545318)
XLA Ops:
  0.6 57.7 %shard_map.148 = (bf16[64,2048]{1,0:T(8,128)(2,1)}, f32[64,2048]{1,0:T(8,128)}, f32[2,16,64,128]{3,2,1,0:T(8,128)}, f32[2,2,8,128]{3,2,1,0:T(8,128)}) custom-call(bf16[64,2048]{1,0:T(8,128)(2,1)} %refs_0_.1, s32[64]{0:T(128)} %refs_1_.1, s32[16,128]{1,0:T(8,128)} %bitcast.4, s32[16,128]{1,0:T(8,128)} %bitcast.5, s32[16,128]{1,0:T(8,128)} %bitcast.6, ...), custom_call_target="tpu_custom_call" | custom-call | tf_op jit(solution)/shard_map/pallas_call | solution.py:808
  58.4 2.5 %shard_map.149 = (bf16[64,2048]{1,0:T(8,128)(2,1)}, f32[64,2048]{1,0:T(8,128)}, f32[64,2048]{1,0:T(8,128)}) custom-call(bf16[64,2048]{1,0:T(8,128)(2,1)} %get-tuple-element.7.filtered_far, f32[64,2048]{1,0:T(8,128)} %get-tuple-element.8.ratio_far, f32[2,16,64,128]{3,2,1,0:T(8,128)} %get-tuple-element.9.lev_far, ...), custom_call_target="tpu_custom_call" | custom-call | tf_op jit(solution)/shard_map/pallas_call | solution.py:891

commit v7 on v6

--- a/solution.py
+++ b/solution.py
@@ -403,7 +403,7 @@
             pr, pi = parts(pq[:half])
             qr, qi = parts(pq[half:])
             re, im = pr - qi, pi + qr
-            tr, ti = parts(turn[pl.ds(pl.multiple_of(e * half, half), half), :])
+            tr, ti = parts(turn[e * half : (e + 1) * half, :])
             y = jnp.concatenate([re * tr - im * ti, re * ti + im * tr], axis=1)
             wr, wi = parts(jnp.dot(across(y), fwd[...], preferred_element_type=F32))
             k = 2 * row + e + rows * lane
@@ -413,7 +413,8 @@
             put(z3, e, 0, half, jnp.concatenate([re * tr + im * ti, im * tr - re * ti], axis=1))
             return c
 
-        lax.fori_loop(0, 2, waves, 0)
+        for e in range(2):
+            waves(e, 0)
 
         back = []
         for e in range(2):

time: 61 us -> 59.9 us (0.982)
  Pallas kernels: 60.2 us -> 59.1 us
    pallas_call x1, Pallas kernels: 57.7 us -> 56.6 us  [body(): pl.pallas_call(functools.partial(kernel, nf, nt), out_shape=(jax.ShapeDty...]
where the time goes in v7:
time: 59.9 us; the launch traced here: 59.7 us
  Pallas kernels  59.1 us (99%)
  between operations  0.64 us (1%)
    pallas_call x1, Pallas kernels, body(): pl.pallas_call(functools.partial(kernel, nf, nt), out_shape=(jax.ShapeDty...  56.6 us
    pallas_call x1, Pallas kernels, body(): pl.pallas_call(finish, out_shape=(jax.ShapeDtypeStruct((HOP, chans), BF16...  2.46 us

profile of v7, /device:TPU:129, one launch (start us, length us, event | category | flops | bytes accessed | tf_op | source)
XLA Modules:
  0.0 59.7 jit_solution(628735988139599612)
XLA Ops:
  0.6 56.6 %shard_map.148 = (bf16[64,2048]{1,0:T(8,128)(2,1)}, f32[64,2048]{1,0:T(8,128)}, f32[2,16,64,128]{3,2,1,0:T(8,128)}, f32[2,2,8,128]{3,2,1,0:T(8,128)}) custom-call(bf16[64,2048]{1,0:T(8,128)(2,1)} %refs_0_.1, s32[64]{0:T(128)} %refs_1_.1, s32[16,128]{1,0:T(8,128)} %bitcast.4, s32[16,128]{1,0:T(8,128)} %bitcast.5, s32[16,128]{1,0:T(8,128)} %bitcast.6, ...), custom_call_target="tpu_custom_call" | custom-call | tf_op jit(solution)/shard_map/pallas_call | solution.py:809
  57.3 2.5 %shard_map.149 = (bf16[64,2048]{1,0:T(8,128)(2,1)}, f32[64,2048]{1,0:T(8,128)}, f32[64,2048]{1,0:T(8,128)}) custom-call(bf16[64,2048]{1,0:T(8,128)(2,1)} %get-tuple-element.7.filtered_far, f32[64,2048]{1,0:T(8,128)} %get-tuple-element.8.ratio_far, f32[2,16,64,128]{3,2,1,0:T(8,128)} %get-tuple-element.9.lev_far, ...), custom_call_target="tpu_custom_call" | custom-call | tf_op jit(solution)/shard_map/pallas_call | solution.py:892
